TPU v7x, 32 devices: a whole 2x2x4 slice. The times are simulated.
32 devices in a mesh: dp: 8 (over z, x), fsdp: 4 (over y, core).
Axes of the slice: x: 2, y: 2, z: 4, core: 2. Of those that a mesh axis runs over, the one named last changes fastest.
Arguments:
- chars: int32 [2, 1024, 6], P(None, ('dp', 'fsdp')), may hold values from 0 to 274
- resets: int32 [2, 1024, 6], P(None, ('dp', 'fsdp')), may hold values 0 or 1
- targets: int32 [2, 1024, 6], P(None, ('dp', 'fsdp')), may hold values from 0 to 274
- embed: bfloat16 [275, 100], replicated, may hold values from -6 to 6
- w_in: bfloat16 [100, 8192], P(None, ('dp', 'fsdp')), may hold values from -0.625 to 0.625
- bias_in: bfloat16 [8192], P(('dp', 'fsdp')), may hold values from -3 to 3
- w_rec: bfloat16 [2048, 8192], P(('dp', 'fsdp')), may hold values from -0.125 to 0.125
- w_dec: bfloat16 [2048, 275], P(('dp', 'fsdp')), may hold values from -0.59765625 to 0.59765625
- bias_dec: bfloat16 [275], replicated, may hold values from -6 to 6
Outputs:
- loss: float32 [], replicated
- hidden: bfloat16 [2, 1024, 6, 2048], P(None, ('dp', 'fsdp'))
- grad_embed: float32 [275, 100], replicated
- grad_w_in: float32 [100, 8192], P(None, ('dp', 'fsdp'))
- grad_bias_in: float32 [8192], P(('dp', 'fsdp'))
- grad_w_rec: float32 [2048, 8192], P(('dp', 'fsdp'))
- grad_w_dec: float32 [2048, 275], P(('dp', 'fsdp'))
- grad_bias_dec: float32 [275], replicated
All inputs are finite; a program needn't handle non-finite values. No bound on the sum of `resets` on one device may be relied on, other than what follows from the above.
Results may differ from a plain program's by a relative error of at most 0.0027.
Values may be sent and summed in bfloat16 or wider, within the bound.
A program may use at most 192 MiB of HBM per device.

v0:
```python
import functools

import jax
import jax.numpy as jnp
from jax import lax
from jax.experimental import pallas as pl
from jax.experimental.pallas import tpu as pltpu
from jax.sharding import PartitionSpec as P

MESH = pl.DeviceIdType.MESH
NN = ((1,), (0,))
NT = ((1,), (1,))
TN = ((0,), (0,))
F32 = jnp.float32
BF = jnp.bfloat16

VPAD = 384
EPAD = 128
RING = 4
SMALL = 112


def mm(left, right, dims):
    return lax.dot_general(left, right, (dims, ((), ())), preferred_element_type=F32)


def sigmoid(v):
    return 0.5 * jnp.tanh(0.5 * v) + 0.5


def lstm_kernel(
    steps, rows,
    w_rec, w_in_raw, b_in_raw, w_dec_raw, emb_raw, bias_raw, chars_in, resets_in, targets_in,
    out_own, out_recv, out_in, out_dec, out_hid, out_small,
    W, WIN, WDEC, IDS, H, HT, HTS, HSEND, A, C, D, DS, DRAW, DL,
    ids_in, w_in, emb_t, w_dec, bias_dec, PR, STG, OWN, DCN, SY, RY, SM, RM, EMBT, LV, BD, GWD, GIS, GY, GM, DWI, IY, SIM, IM, RS1, RS2, RS3, RS4, RS5, PIECE, TOTAL,
    s_ids, r_ids, s_win, r_win, s_wa, r_wa, s_wm, r_wm, s_wy, r_wy, s_ws, r_ws,
    s_da, r_da, s_dm, r_dm, s_dy, r_dy, s_ds, r_ds, s_h, r_h, s_ht, r_ht, s_d, r_d,
    s_pr, r_pr, s_gd, r_gd, s_gi, r_gi, s_sm, r_sm, s_ry, r_ry, s_rm, r_rm, s_ra, r_ra,
    l_sem, hid_sem,
):
    last = steps - 1
    dp, fs = lax.axis_index("dp"), lax.axis_index("fsdp")
    z, x, y, c = dp // 2, dp % 2, fs // 2, fs % 2
    zh = z // 2
    a = z + zh * (3 - 2 * z)

    def dev(zz, xx, yy, cc):
        return (zz * 2 + xx, yy * 2 + cc)

    def kx(k):
        return x + (k % 2) * (1 - 2 * x)

    def kz(k):
        return z + (k // 2) * (1 - 2 * (z % 2))

    def ka(k):
        return a + (k // 2) * (1 - 2 * a)

    def kdev(k):
        return dev(kz(k), kx(k), y, c)

    def member(k):
        return 2 * kx(k) + ka(k)

    def unit_block(k, j):
        return 2 * (ka(k) + j * (3 - 2 * ka(k))) + kx(k)

    def lanes(ub):
        return pl.ds(pl.multiple_of(256 * ub, 256), 256)

    def place(k, far, yy, cc):
        return 4 * (2 * k + zh + far * (1 - 2 * zh)) + 2 * yy + cc

    def span(k, j):
        return slice(256 * (2 * k + j), 256 * (2 * k + j + 1))

    mir, ydev, sib = dev(3 - z, x, y, c), dev(z, x, 1 - y, c), dev(z, x, y, 1 - c)
    cross = dev(3 - z, x, 1 - y, c)
    perm = dev(2 * x + y, c, z // 2, z % 2)
    back = dev(2 * y + c, z // 2, z % 2, x)
    stays = jnp.logical_and(perm[0] == dp, perm[1] == fs)
    moved = jnp.logical_not(stays)

    def rc(src, dst, ss, rs, to):
        return pltpu.make_async_remote_copy(
            src_ref=src, dst_ref=dst, send_sem=ss, recv_sem=rs, device_id=to, device_id_type=MESH
        )

    emb, vocab = emb_raw.shape[1], emb_raw.shape[0]
    w_in[...] = jnp.zeros_like(w_in)
    w_in[0:emb, :] = w_in_raw[...]
    tail = emb // 16 * 16
    part = w_in[tail : tail + 16, :].astype(F32)
    bias_row = b_in_raw[...].astype(F32).reshape(1, 256)
    part = jnp.where(lax.broadcasted_iota(jnp.int32, (16, 256), 0) == emb - tail, bias_row, part)
    w_in[tail : tail + 16, :] = part.astype(BF)
    for s in range(2):
        stack = jnp.concatenate(
            [v for ref in (chars_in, resets_in, targets_in) for v in (ref[:, s, :], jnp.zeros((8 - steps, 32), jnp.int32))],
            axis=0,
        ).astype(F32)
        wide_stack = jnp.concatenate([stack, jnp.zeros((24, 96), F32)], axis=1)
        ids_in[s] = wide_stack.T[:32, :].astype(jnp.int32)
    barrier = pltpu.get_barrier_semaphore()

    def greet(to):
        pl.semaphore_signal(barrier, inc=1, device_id=to, device_id_type=MESH)

    for k in (1, 2, 3):
        greet(kdev(k))
    for to in (mir, ydev, sib, cross):
        greet(to)

    @pl.when(moved)
    def _():
        greet(perm)
        greet(back)

    pl.semaphore_wait(barrier, 7 + 2 * moved.astype(jnp.int32))


    def d_slot(b):
        return WDEC.at[pl.ds(pl.multiple_of(64 * b, 64), 64), :]

    def w_cols(ub, g):
        return w_rec.at[:, lanes(8 * g + ub)]

    def w_part(j, g, b):
        return W.at[4 * j + g, pl.ds(pl.multiple_of(64 * b, 64), 64), :]

    def wa_start(k):
        for j in (0, 1):
            for g in range(4):
                rc(w_cols(unit_block(k, j), g), w_part(j, g, place(k, 0, y, c)), s_wa.at[k - 1, j], r_wa.at[k - 1, j], kdev(k)).start()

    def wa(k, j):
        b = place(k, 0, y, c)
        part = W.at[pl.ds(4 * j, 4), pl.ds(pl.multiple_of(64 * b, 64), 64), :]
        return rc(part, part, s_wa.at[k - 1, j], r_wa.at[k - 1, j], kdev(k))

    def ids_copy(k, mem):
        return rc(ids_in, IDS.at[:, mem], s_ids.at[k - 1], r_ids.at[k - 1], kdev(k))

    def own_w(j, g):
        return pltpu.make_async_copy(w_cols(unit_block(0, j), g), w_part(j, g, place(0, 0, y, c)), l_sem.at[4 * j + g])

    for j in (0, 1):
        for g in range(4):
            own_w(j, g).start()
    for k in (1, 2, 3):
        ids_copy(k, member(0)).start()

    def win_perm(jj, gy, gc):
        return rc(w_in, WIN.at[jj, gy, gc], s_win.at[0], r_win.at[0], perm)

    def win_local():
        return pltpu.make_async_copy(w_in, WIN.at[x, z // 2, z % 2], l_sem.at[8])

    @pl.when(moved)
    def _():
        win_perm(x, z // 2, z % 2).start()

    @pl.when(stays)
    def _():
        win_local().start()

    for k in (1, 2, 3):
        wa_start(k)

    def w_half(j, b):
        return W.at[pl.ds(4 * j, 4), pl.ds(pl.multiple_of(64 * b, 64), 64), :]

    def to_mir(k, j):
        b = place(k, 0, y, c)
        return rc(w_half(j, b), w_half(j, b), s_wm.at[k, j], r_wm.at[k, j], mir)

    def from_mir(k, j):
        b = place(k, 1, y, c)
        return rc(w_half(j, b), w_half(j, b), s_wm.at[k, j], r_wm.at[k, j], mir)

    def group_block(i, yy, cc):
        return place(i % 4, i // 4, yy, cc)

    def to_y(i, j):
        b = group_block(i, y, c)
        return rc(w_half(j, b), w_half(j, b), s_wy.at[i, j], r_wy.at[i, j], ydev)

    def from_y(i, j):
        b = group_block(i, 1 - y, c)
        return rc(w_half(j, b), w_half(j, b), s_wy.at[i, j], r_wy.at[i, j], ydev)

    def to_s(i, j):
        b = group_block(i % 8, y + (i // 8) * (1 - 2 * y), c)
        return rc(w_half(j, b), w_half(j, b), s_ws.at[i, j], r_ws.at[i, j], sib)

    def from_s(i, j):
        b = group_block(i % 8, y + (i // 8) * (1 - 2 * y), 1 - c)
        return rc(w_half(j, b), w_half(j, b), s_ws.at[i, j], r_ws.at[i, j], sib)

    for j in (0, 1):
        for g in range(4):
            own_w(j, g).wait()
    inner = a == 1

    @pl.when(inner)
    def _():
        for j in (0, 1):
            to_mir(0, j).start()

    for j in (0, 1):
        to_y(0, j).start()
        to_s(0, j).start()

    def win_mir(jj):
        return rc(WIN.at[jj, y, c], WIN.at[jj, y, c], s_win.at[1], r_win.at[1], mir)

    def win_y(yy):
        return rc(WIN.at[:, yy, c], WIN.at[:, yy, c], s_win.at[2], r_win.at[2], ydev)

    def win_s(cc):
        return rc(WIN.at[:, :, cc], WIN.at[:, :, cc], s_win.at[3], r_win.at[3], sib)

    @pl.when(moved)
    def _():
        win_perm(zh, y, c).wait_recv()

    @pl.when(stays)
    def _():
        win_local().wait()

    win_mir(zh).start()


    IDS[:, member(0)] = ids_in[...]

    def own_blocks(k):
        for j in (0, 1):
            wa(k, j).wait_recv()
            to_y(k, j).start()

            @pl.when(inner)
            def _(j=j):
                to_mir(k, j).start()

            to_s(k, j).start()

    own_blocks(1)
    own_blocks(2)
    own_blocks(3)

    def da(k):
        return rc(w_dec, d_slot(place(k, 0, y, c)), s_da.at[k - 1], r_da.at[k - 1], kdev(k))

    HSEND[0, 0 : VPAD // 128] = jnp.zeros((VPAD // 128, 128, rows), BF)
    for n in range(VPAD // 128):
        held = min(128, vocab - 128 * n)
        HSEND[0, n, 0:held, 0:emb] = emb_raw[128 * n : 128 * n + held, :]
    unit = jnp.where(
        lax.broadcasted_iota(jnp.int32, (EPAD, EPAD), 0) == lax.broadcasted_iota(jnp.int32, (EPAD, EPAD), 1), 1.0, 0.0
    ).astype(BF)
    turned = mm(unit, HSEND[0, 0 : VPAD // 128].reshape(VPAD, EPAD), NT)
    emb_t[...] = jnp.where(lax.broadcasted_iota(jnp.int32, (EPAD, VPAD), 0) == emb, 1.0, turned).astype(BF)
    w_dec[...] = jnp.zeros_like(w_dec)
    w_dec[:, :vocab] = w_dec_raw[...]
    bias_dec[...] = jnp.full_like(bias_dec, -1e30)
    bias_dec[0:1, :vocab] = bias_raw[...].astype(F32).reshape(1, vocab)
    for k in (1, 2, 3):
        da(k).start()
    own_dec = pltpu.make_async_copy(w_dec, d_slot(place(0, 0, y, c)), l_sem.at[9])
    own_dec.start()

    for k in (1, 2, 3):
        ids_copy(k, member(k)).wait_recv()
    lane = lax.broadcasted_iota(jnp.int32, (rows, 24), 1)
    wide = lax.broadcasted_iota(jnp.int32, (rows, VPAD), 1).astype(F32)

    def column(at, s):
        packed = IDS[s].reshape(rows, 24)
        return jnp.sum(jnp.where(lane == at, packed, 0).astype(F32), axis=1, keepdims=True)

    def keep_of(t, s):
        return 1.0 - column(8 + t, s)

    def letter(t, s):
        return jnp.where(column(t, s) == wide, 1.0, 0.0).astype(BF)

    EMBT[...] = jnp.zeros_like(EMBT)
    LV[...] = jnp.zeros_like(LV)
    BD[...] = jnp.zeros_like(BD)
    GWD[...] = jnp.zeros_like(GWD)
    DWI[...] = jnp.zeros_like(DWI)
    DCN[...] = jnp.zeros_like(DCN)
    OWN[...] = jnp.zeros_like(OWN)
    PR[0] = jnp.zeros(PR.shape[1:], BF)

    win_mir(1 - zh).wait_recv()

    win_y(y).start()
    def pass_y(i):
        for j in (0, 1):
            from_y(i, j).wait_recv()
            to_s(8 + i, j).start()

    def pass_mir(k):
        for j in (0, 1):
            from_mir(k, j).wait_recv()
            to_y(4 + k, j).start()
            to_s(4 + k, j).start()

    for i in range(3):
        pass_y(i)

    @pl.when(inner)
    def _():
        pass_mir(0)

    @pl.when(jnp.logical_not(inner))
    def _():
        for k in range(4):
            for j in (0, 1):
                to_mir(k, j).start()

    pass_y(3)
    win_y(1 - y).wait_recv()
    win_s(c).start()
    win_s(1 - c).wait_recv()

    def h_copy(t, s, k, j):
        src, dst = H.at[t % RING, s, :, span(0, j)], H.at[t % RING, s, :, span(k, j)]
        return rc(src, dst, s_h.at[t, s, k - 1, j], r_h.at[t, s, k - 1, j], kdev(k))

    def wait_h(t, s):
        for k in (1, 2, 3):
            for j in (0, 1):
                h_copy(t, s, k, j).wait_recv()

    def gates(t, s, first):
        keep = None if first else keep_of(t, s)
        feature = mm(letter(t, s), emb_t[...], NT).astype(BF)
        for j in (0, 1):
            pre = []
            for g in range(4):
                drive = mm(feature, WIN[j, g // 2, g % 2], NN)
                if not first:
                    drive = drive + keep * mm(H[(t - 1) % RING, s], W[4 * j + g], NN)
                pre.append(drive)
            s_i, s_f, t_g, s_o = sigmoid(pre[0]), sigmoid(pre[1]), jnp.tanh(pre[2]), sigmoid(pre[3])
            cell = s_i * t_g
            if not first:
                cell = s_f * (C[t - 1, s, j] * keep) + cell
            for g, v in enumerate((s_i, s_f, t_g, s_o)):
                A[t, s, 4 * j + g] = v
            C[t, s, j] = cell
            H[t % RING, s, :, span(0, j)] = (s_o * jnp.tanh(cell)).astype(BF)
            for k in (3, 1, 2):
                h_copy(t, s, k, j).start()

    @pl.loop(0, 2)
    def _(s):
        gates(0, s, True)

    @pl.when(jnp.logical_not(inner))
    def _():
        pass_mir(0)

    for k in (1, 2, 3):
        pass_mir(k)

    def dec_mir(k, far):
        b = place(k, far, y, c)
        return rc(d_slot(b), d_slot(b), s_dm.at[k], r_dm.at[k], mir)

    def dec_y(i, yy):
        b = group_block(i, yy, c)
        return rc(d_slot(b), d_slot(b), s_dy.at[i], r_dy.at[i], ydev)

    def dec_s(i, cc):
        b = group_block(i % 8, y + (i // 8) * (1 - 2 * y), cc)
        return rc(d_slot(b), d_slot(b), s_ds.at[i], r_ds.at[i], sib)

    own_dec.wait()
    dec_mir(0, 0).start()
    dec_y(0, y).start()
    dec_s(0, c).start()
    for k in (1, 2, 3):
        da(k).wait_recv()
        dec_mir(k, 0).start()
        dec_y(k, y).start()
        dec_s(k, c).start()

    for i in (4, 5, 6, 7):
        pass_y(i)

    @pl.loop(0, 16)
    def _(i):
        for j in (0, 1):
            from_s(i, j).wait_recv()

    def released(t, s):
        hid_copy(t, s).wait()
        for k in (1, 2, 3):
            for j in (0, 1):
                h_copy(t, s, k, j).wait_send()

    def forward(t, s):
        wait_h(t - 1, s)

        @pl.when(t >= RING - 1)
        def _():
            released(t - (RING - 1), s)

        gates(t, s, False)

    row = lax.broadcasted_iota(jnp.int32, (128, 256), 0)
    col = lax.broadcasted_iota(jnp.int32, (128, 256), 1)

    def select(cc):
        yy = y + (row // 64) * (1 - 2 * y)
        return jnp.where(col == 64 * (2 * yy + cc) + row % 64, 1.0, 0.0).astype(BF)

    def lane_slot(t, s):
        return pl.ds(pl.multiple_of((2 * t + s) * rows, rows), rows)

    def ht_copy(t, s, slot):
        return rc(HSEND.at[slot], HTS.at[:, :, lane_slot(t, s)], s_ht.at[t, s], r_ht.at[t, s], sib)

    def hid_copy(t, s):
        mine = H.at[t % RING, s, pl.ds(pl.multiple_of(32 * member(0), 32), 32), :]
        return pltpu.make_async_copy(mine, out_hid.at[s * steps + t], hid_sem.at[t, s])

    def logits_of(t, s):
        scores = mm(H[t % RING, s], WDEC[...], NN) + bias_dec[0:1, :]
        top = jnp.max(scores, axis=1, keepdims=True)
        shifted = jnp.exp(scores - top)
        summed = jnp.sum(shifted, axis=1, keepdims=True)
        goal = jnp.where(column(16 + t, s) == wide, 1.0, 0.0)
        picked = jnp.sum(goal * scores, axis=1, keepdims=True)
        LV[...] += jnp.broadcast_to(top + jnp.log(summed) - picked, (rows, 128))
        DL[t, s] = (shifted / summed - goal).astype(BF)

    def decoder_side(t, s):
        hid_copy(t, s).start()
        grad = DL[t, s]
        BD[...] += mm(jnp.ones((8, rows), BF), grad, NN)
        for j in (0, 1):
            GWD[j] += mm(H[t % RING, s, :, span(0, j)], grad, TN).reshape(2, 2, 64, VPAD)

    def transposed_side(t, s):
        slot = s
        mine, other = select(c), select(1 - c)

        @pl.when(t >= 1)
        def _():
            ht_copy(t - 1, s, slot).wait_send()

        for tile in range(8):
            part = H[t % RING, s, :, 256 * tile : 256 * (tile + 1)]
            HT[tile, :, lane_slot(t, s)] = mm(mine, part, NT).astype(BF)
            HSEND[slot, tile] = mm(other, part, NT).astype(BF)
        ht_copy(t, s, slot).start()

    def decoder_mirror():
        @pl.loop(0, 4)
        def _(k):
            dec_mir(k, 1).wait_recv()
            dec_y(4 + k, y).start()
            dec_s(4 + k, c).start()

    def decoder_rest():
        @pl.loop(0, 8)
        def _(i):
            k, j = i // 2, i % 2
            to_mir(k, j).wait_send()
            to_y(i, 0).wait_send()
            to_y(i, 1).wait_send()

        @pl.loop(0, 16)
        def _(i):
            to_s(i, 0).wait_send()
            to_s(i, 1).wait_send()

        @pl.loop(0, 8)
        def _(i):
            dec_y(i, 1 - y).wait_recv()
            dec_s(8 + i, c).start()

        @pl.loop(0, 16)
        def _(i):
            dec_s(i, 1 - c).wait_recv()

    def aside(t, s):
        logits_of(t, s)
        decoder_side(t, s)
        transposed_side(t, s)

    @pl.loop(2, 2 * steps)
    def _(i):
        t, s = i // 2, i % 2
        forward(t, s)

        @pl.when(i == 3)
        def _():
            decoder_mirror()

        @pl.when(i == 5)
        def _():
            decoder_rest()

        @pl.when(i >= 5)
        def _():
            @pl.loop(i - 4 - (13 - i) // 8, i - 3)
            def _(n):
                aside(n // 2, n % 2)

    def pr_copy(t, s, k, j):
        return rc(STG.at[s, k - 1, j], PR.at[t % 2, s, k - 1, j], s_pr.at[t, s, k - 1, j], r_pr.at[t, s, k - 1, j], kdev(k))

    def d_copy(t, s):
        return rc(D.at[:, t - 1, s], DS.at[:, t - 1, s], s_d.at[t, s], r_d.at[t, s], sib)

    def turn():
        def rows_of(q):
            return pl.ds(pl.multiple_of(256 * q, 256), 256)

        def swap(p, q):
            upper, lower = W[p, rows_of(q), :].T, W[q, rows_of(p), :].T
            W[p, rows_of(q), :] = lower
            W[q, rows_of(p), :] = upper

        @pl.loop(0, 8)
        def _(p):
            W[p, rows_of(p), :] = W[p, rows_of(p), :].T
            for step in (1, 2, 3):
                swap(p, (p + step) % 8)

        @pl.loop(0, 4)
        def _(p):
            swap(p, p + 4)

    def cell_back(t, s, oldest):
        keep = keep_of(t, s)
        for j in (0, 1):
            up = WDEC[span(0, j), :]
            dh = mm(DL[t, s], up, NT)
            rest = PR[(t + 1) % 2, s, 0, j].astype(F32) + PR[(t + 1) % 2, s, 1, j].astype(F32)
            rest = rest + PR[(t + 1) % 2, s, 2, j].astype(F32)
            dh = dh + (OWN[s, j] + rest)
            s_i, s_f, t_g, s_o = (A[t, s, 4 * j + g] for g in range(4))
            t_c = jnp.tanh(C[t, s, j])
            d_o = dh * t_c
            d_c = dh * s_o * (1.0 - t_c * t_c) + DCN[s, j]
            d_i = d_c * t_g * s_i * (1.0 - s_i)
            d_g = d_c * s_i * (1.0 - t_g * t_g)
            d_o = d_o * s_o * (1.0 - s_o)
            if oldest:
                d_f = jnp.zeros_like(d_i)
            else:
                d_f = d_c * (C[t - 1, s, j] * keep) * s_f * (1.0 - s_f)
                DCN[s, j] = keep * (d_c * s_f)
            for g, v in enumerate((d_i, d_f, d_g, d_o)):
                low = v.astype(BF)
                DRAW[4 * j + g] = low
                if not oldest:
                    D[4 * j + g, t - 1, s] = low * keep.astype(BF)

    def pr_each(act):
        for k in (3, 1, 2):
            for j in (0, 1):
                act(k, j)

    def product_back(t, s):
        left = jnp.concatenate([D[q, t - 1, s] for q in range(8)], axis=1)
        for k in (3, 1, 2, 0):
            for j in (0, 1):
                total = mm(left, W[2 * k + j], NN)
                if k == 0:
                    OWN[s, j] = total
                else:
                    STG[s, k - 1, j] = total.astype(BF)
        pr_each(lambda k, j: pr_copy(t, s, k, j).start())

    def input_side(t, s):
        onehot = letter(t, s)
        feat_t = mm(emb_t[...], onehot, NT).astype(BF)
        inputs = []
        for q in range(8):
            jj, gy, gc = q // 4, (q // 2) % 2, q % 2
            DWI[jj, gy, gc] += mm(feat_t, DRAW[q], NN)
            inputs.append(WIN[jj, gy, gc])
        grad_t = mm(jnp.concatenate(inputs, axis=1), jnp.concatenate([DRAW[q] for q in range(8)], axis=1), NT)
        high = grad_t.astype(BF)
        low = (grad_t - high.astype(F32)).astype(BF)
        EMBT[...] += mm(high, onehot, NN) + mm(low, onehot, NN)

    def gd_s():
        return rc(GWD.at[:, :, 1 - c], GIS.at[:, :, 0:64], s_gd.at[0], r_gd.at[0], sib)

    def gd_y():
        return rc(GWD.at[:, 1 - y, c], GY, s_gd.at[1], r_gd.at[1], ydev)

    def gd_m():
        return rc(GWD.at[1 - zh, y, c], GM, s_gd.at[2], r_gd.at[2], mir)

    @pl.loop(0, 2 * (steps - 1))
    def _(i):
        t, s = last - i // 2, i % 2

        @pl.when(i < 2)
        def _():
            wait_h(last, s)
            logits_of(last, s)

        @pl.when(i >= 2)
        def _():
            pr_each(lambda k, j: pr_copy(t + 1, s, k, j).wait_recv())

        cell_back(t, s, False)
        d_copy(t, s).start()

        @pl.when(i >= 2)
        def _():
            pr_each(lambda k, j: pr_copy(t + 1, s, k, j).wait_send())

        @pl.when(i == 0)
        def _():
            turn()

        product_back(t, s)
        input_side(t, s)

        @pl.when(i < 2)
        def _():
            aside(last - 1, s)

        @pl.when(i == 3)
        def _():
            @pl.loop(0, 2)
            def _(n):
                decoder_side(last, n)

            gd_s().start()

        @pl.when(i == 4)
        def _():
            gd_s().wait_recv()
            GWD[:, :, c] += GIS[:, :, 0:64]
            gd_y().start()

        @pl.when(i == 6)
        def _():
            gd_y().wait_recv()
            GWD[:, y, c] += GY[...]
            gd_m().start()

        @pl.when(i == 8)
        def _():
            gd_m().wait_recv()
            out_dec[...] = GWD[zh, y, c] + GM[...]

    @pl.loop(0, 2 * (steps - 1))
    def _(i):
        ht_copy(i // 2, i % 2, 0).wait_recv()
        d_copy(1 + i // 2, i % 2).wait_recv()

    depth = 2 * (steps - 1) * rows

    def kept(q):
        return A.at[2 + q // 4, (q % 4) // 2, :, pl.ds(pl.multiple_of(64 * (q % 2), 64), 64), :]

    def tile_of(q):
        k, near = q % 4, q // 4
        return 2 * k + 1 - zh + near * (2 * zh - 1)

    def ry_copy(p, q):
        return rc(SY.at[p % 4], RY.at[q], s_ry.at[p], r_ry.at[q], ydev)

    def rm_copy(k):
        return rc(SM.at[k], RM.at[k], s_rm.at[k], r_rm.at[k], mir)

    def half(h):
        return pl.ds(4 * h, 4)

    def ry_half(h):
        return rc(SY.at[0, half(h)], RY.at[3, half(h)], s_ry.at[8 + h], r_ry.at[8 + h], ydev)

    def rm_half(h):
        return rc(SM.at[3, half(h)], RM.at[3, half(h)], s_rm.at[4 + h], r_rm.at[4 + h], mir)

    def ry_sent(p):
        @pl.when(p == 0)
        def _():
            ry_half(0).wait_send()
            ry_half(1).wait_send()

        @pl.when(p > 0)
        def _():
            ry_copy(p, order(p)).wait_send()

    def rm_sent(k):
        if k == 3:
            rm_half(0).wait_send()
            rm_half(1).wait_send()
        else:
            rm_copy(k).wait_send()

    def ra_copy(k):
        return rc(SM.at[k], out_recv.at[k - 1], s_ra.at[k - 1], r_ra.at[k - 1], kdev(k))

    def order(p):
        return 3 - p + 8 * (p // 4)

    def make_tile(p):
        q = order(p)
        tile = tile_of(q)
        left, right = HT[tile], HTS[tile]
        hold = kept(q)

        @pl.when(p >= 4)
        def _():
            ry_sent(p - 4)

        for n in range(8):
            grad = mm(left, D[n].reshape(depth, 256), NN) + mm(right, DS[n].reshape(depth, 256), NN)
            hold[n] = grad[:64]
            SY[p % 4, n] = grad[64:].astype(BF)
            if n % 4 == 3:
                @pl.when(p == 0)
                def _(n=n):
                    ry_half(n // 4).start()

        @pl.when(p > 0)
        def _():
            ry_copy(p, q).start()

    def add_y(q):
        ry_copy(0, q).wait_recv()
        hold = kept(q)
        hold[...] = hold[...] + RY[q].astype(F32)

    def pass_on(k):
        if k == 3:
            hold = kept(k)
            for h in (0, 1):
                ry_half(h).wait_recv()
                SM[3, half(h)] = (hold[half(h)] + RY[3, half(h)].astype(F32)).astype(BF)
                rm_half(h).start()
            return
        add_y(k)
        SM[k] = kept(k)[...].astype(BF)
        rm_copy(k).start()

    def finish(k):
        add_y(4 + k)
        if k == 3:
            rm_half(0).wait_recv()
            rm_half(1).wait_recv()
        else:
            rm_copy(k).wait_recv()
        total = kept(4 + k)[...] + RM[k].astype(F32)
        if k == 0:
            out_own[...] = total
        else:
            rm_sent(k)
            SM[k] = total.astype(BF)
            ra_copy(k).start()

    def settle(p):
        q = order(p)
        pass_on(q) if q < 4 else finish(q - 4)

    outer = jnp.logical_not(inner)

    def core_rows(cc):
        return pl.ds(pl.multiple_of(64 * cc, 64), 64)

    def piece_rows(xx):
        return pl.ds(pl.multiple_of(64 * c + 32 * xx, 32), 32)

    def sm_core():
        return rc(out_small.at[core_rows(1 - c)], RS1, s_sm.at[0], r_sm.at[0], sib)

    def sm_group(k):
        xx = kx(k)
        return rc(out_small.at[piece_rows(xx)], RS2.at[k - 1], s_sm.at[k], r_sm.at[k], kdev(k))

    def sm_quarter(n):
        return rc(PIECE, RS3.at[n], s_sm.at[4 + n], r_sm.at[4 + n], (ydev, mir, cross)[n])

    def sm_spread(k):
        return rc(TOTAL, RS4.at[k - 1], s_sm.at[6 + k], r_sm.at[6 + k], kdev(k))

    def sm_last():
        return rc(out_small.at[core_rows(c)], RS5, s_sm.at[10], r_sm.at[10], sib)

    def sm_step1():
        sm_core().wait_recv()
        out_small[core_rows(c)] = out_small[core_rows(c)] + RS1[...]

        @pl.when(outer)
        def _():
            sm_group(1).start()

        @pl.when(inner)
        def _():
            sm_group(2).start()
            sm_group(3).start()

    def sm_step2():
        @pl.when(outer)
        def _():
            for k in (1, 2, 3):
                sm_group(k).wait_recv()
            PIECE[...] = (out_small[piece_rows(x)] + RS2[0]) + (RS2[1] + RS2[2])
            for n in range(3):
                sm_quarter(n).start()

    def sm_step3():
        @pl.when(outer)
        def _():
            for n in range(3):
                sm_quarter(n).wait_recv()
            TOTAL[...] = (PIECE[...] + RS3[0]) + (RS3[1] + RS3[2])
            for k in (1, 2, 3):
                sm_spread(k).start()

    def sm_step4():
        sm_core().wait_send()

        @pl.when(outer)
        def _():
            sm_group(1).wait_send()
            sm_spread(1).wait_recv()
            out_small[piece_rows(1 - x)] = RS4[0]
            out_small[piece_rows(x)] = TOTAL[...]

        @pl.when(inner)
        def _():
            for k in (2, 3):
                sm_group(k).wait_send()
                sm_spread(k).wait_recv()
                out_small[piece_rows(kx(k))] = RS4[k - 1]

        sm_last().start()

    def sm_step5():
        sm_last().wait_recv()
        out_small[core_rows(1 - c)] = RS5[...]

    live = pl.ds(0, 104)

    def gi_s():
        return rc(DWI.at[:, :, 1 - c, live], GIS.at[:, :, :, 0:256], s_gi.at[0], r_gi.at[0], sib)

    def gi_y():
        return rc(DWI.at[:, 1 - y, c, live], IY, s_gi.at[1], r_gi.at[1], ydev)

    def gi_m():
        return rc(SIM, IM, s_gi.at[2], r_gi.at[2], mir)

    def gi_p():
        return rc(DWI.at[zh, y, c, live], out_in, s_gi.at[3], r_gi.at[3], back)

    def first_position():
        @pl.loop(0, 2)
        def _(s):
            pr_each(lambda k, j: pr_copy(1, s, k, j).wait_recv())
            cell_back(0, s, True)
            input_side(0, s)

        leader = jnp.logical_and(x == 0, a == 0)
        high_row = lax.broadcasted_iota(jnp.int32, (8, VPAD), 0)
        loss = jnp.sum(LV[...], axis=0, keepdims=True)
        loss = jnp.concatenate([loss] * (VPAD // 128), axis=1)
        extra = jnp.where(high_row == 0, BD[...], jnp.where(high_row == 1, loss, 0.0))
        out_small[...] = EMBT[...]
        out_small[SMALL - 8 : SMALL] = jnp.where(leader, extra, 0.0)
        sm_core().start()
        gi_s().start()

    @pl.loop(0, 8)
    def _(p):
        make_tile(p)

        @pl.when(p == 1)
        def _():
            @pl.when(inner)
            def _():
                settle(0)

            first_position()
            sm_step1()
            gi_s().wait_recv()
            DWI[:, :, c, 0:104] = DWI[:, :, c, 0:104] + GIS[:, :, :, 0:256]
            gi_y().start()

            @pl.when(outer)
            def _():
                settle(0)

        @pl.when(p == 2)
        def _():
            settle(1)

        @pl.when(p == 3)
        def _():
            gi_y().wait_recv()
            DWI[:, y, c, 0:104] = DWI[:, y, c, 0:104] + IY[...]
            SIM[...] = DWI[1 - zh, y, c, 0:112].astype(BF)
            gi_m().start()

        @pl.when(p == 4)
        def _():
            settle(2)

        @pl.when(p == 5)
        def _():
            settle(3)

    sm_step2()
    settle(4)
    settle(5)
    settle(6)
    sm_step3()
    gi_m().wait_recv()
    DWI[zh, y, c, 0:104] = DWI[zh, y, c, 0:104] + IM[...].astype(F32)[0:104]

    @pl.when(moved)
    def _():
        gi_p().start()

    @pl.when(stays)
    def _():
        out_in[...] = DWI[zh, y, c, 0:104]

    sm_step4()
    settle(7)
    sm_step5()

    for k in (1, 2, 3):
        for j in (0, 1):
            wa(k, j).wait_send()
            for s in range(2):
                pr_copy(1, s, k, j).wait_send()
        ids_copy(k, member(0)).wait_send()
        da(k).wait_send()
        ra_copy(k).wait()
    rm_copy(0).wait_send()

    @pl.when(moved)
    def _():
        gi_p().wait()
        win_perm(x, z // 2, z % 2).wait_send()

    win_mir(zh).wait_send()
    win_y(y).wait_send()
    win_s(c).wait_send()
    @pl.when(outer)
    def _():
        for k in (1, 2, 3):
            sm_quarter(k - 1).wait_send()
            sm_spread(k).wait_send()

    for copy in (gd_s, gd_y, gd_m, gi_s, gi_y, gi_m, sm_last):
        copy().wait_send()
    for s in range(2):
        ht_copy(last - 1, s, s).wait_send()

    @pl.loop(0, 4)
    def _(k):
        dec_mir(k, 0).wait_send()

    @pl.loop(0, 8)
    def _(i):
        dec_y(i, y).wait_send()

    for p in range(4, 8):
        ry_copy(p, order(p)).wait_send()

    @pl.loop(0, 16)
    def _(i):
        dec_s(i, c).wait_send()

    @pl.loop(2 * (steps - RING + 1), 2 * steps)
    def _(i):
        released(i // 2, i % 2)

    @pl.loop(0, 2 * (steps - 1))
    def _(i):
        d_copy(1 + i // 2, i % 2).wait_send()


def output_kernel(
    own, recv, g_in, g_dec, hid_in, small, hid, table, o_in, o_bias, o_rec, o_dec, o_bias_dec, loss,
    h_buf, own_buf, recv_buf, rec_buf, in_sem, out_sem,
):
    dp = lax.axis_index("dp")
    z, x = dp // 2, dp % 2
    a = z + (z // 2) * (3 - 2 * z)
    parts = 8

    def cols(k, j, g):
        xk, ak = x + (k % 2) * (1 - 2 * x), a + (k // 2) * (1 - 2 * a)
        ub = 2 * (ak + j * (3 - 2 * ak)) + xk
        return pl.ds(pl.multiple_of(256 * (8 * g + ub), 256), 256)

    def hid_load(p):
        return pltpu.make_async_copy(hid_in.at[:, :, 256 * p : 256 * (p + 1)], h_buf.at[:, :, cols(p // 2, p % 2, 0)], in_sem.at[p])

    def hid_store():
        return pltpu.make_async_copy(h_buf, hid, out_sem.at[1])

    def rec_load(k):
        if k == 0:
            return pltpu.make_async_copy(own, own_buf, in_sem.at[parts])
        return pltpu.make_async_copy(recv.at[k - 1], recv_buf.at[k - 1], in_sem.at[parts + k])

    for p in range(parts):
        hid_load(p).start()
    for k in range(4):
        rec_load(k).start()
    for p in range(parts):
        hid_load(p).wait()
    hid_store().start()
    vocab, emb = table.shape
    table[...] = small[0:SMALL, :].T[:vocab, :emb]
    o_in[...] = g_in[0:emb, :]
    o_bias[...] = g_in[emb, :]
    o_dec[...] = g_dec[:, :vocab]
    o_bias_dec[...] = small[SMALL - 8, :vocab]
    loss[...] = small[SMALL - 7 : SMALL - 6, 0:1]
    for k in range(4):
        rec_load(k).wait()
        for j in (0, 1):
            for g in range(4):
                part = own_buf[4 * j + g] if k == 0 else recv_buf[k - 1, 4 * j + g].astype(F32)
                rec_buf[:, cols(k, j, g)] = part
    rec_store = pltpu.make_async_copy(rec_buf, o_rec, out_sem.at[0])
    rec_store.start()
    rec_store.wait()
    hid_store().wait()


def fused(chars, resets, targets, embed, w_in, bias_in, w_rec, w_dec, bias_dec):
    micro, count, steps = chars.shape
    own_rows, gate_cols = w_rec.shape
    vocab, emb = embed.shape
    width = gate_cols // 4
    members = 4
    rows = count * members
    vm = pl.BlockSpec(memory_space=pltpu.VMEM)
    hbm = pl.BlockSpec(memory_space=pl.ANY)
    dma = pltpu.SemaphoreType.DMA
    n = steps - 1
    scratch = [
        pltpu.VMEM((8, width, 256), BF),
        pltpu.VMEM((2, 2, 2, EPAD, 256), BF),
        pltpu.VMEM((width, VPAD), BF),
        pltpu.VMEM((micro, members, count, 24), jnp.int32),
        pltpu.VMEM((RING, micro, rows, width), BF),
        pltpu.VMEM((8, 128, 2 * n * rows), BF),
        pltpu.VMEM((8, 128, 2 * n * rows), BF),
        pltpu.VMEM((2, 8, 128, rows), BF),
        pltpu.VMEM((steps, micro, 8, rows, 256), F32),
        pltpu.VMEM((steps, micro, 2, rows, 256), F32),
        pltpu.VMEM((8, n, micro, rows, 256), BF),
        pltpu.VMEM((8, n, micro, rows, 256), BF),
        pltpu.VMEM((8, rows, 256), BF),
        pltpu.VMEM((steps, micro, rows, VPAD), BF),
        pltpu.VMEM((micro, count, 24), jnp.int32),
        pltpu.VMEM((EPAD, 256), BF),
        pltpu.VMEM((EPAD, VPAD), BF),
        pltpu.VMEM((own_rows, VPAD), BF),
        pltpu.VMEM((8, VPAD), F32),
        pltpu.VMEM((2, micro, 3, 2, rows, 256), BF),
        pltpu.VMEM((micro, 3, 2, rows, 256), BF),
        pltpu.VMEM((micro, 2, rows, 256), F32),
        pltpu.VMEM((micro, 2, rows, 256), F32),
        pltpu.VMEM((4, 8, 64, 256), BF),
        pltpu.VMEM((8, 8, 64, 256), BF),
        pltpu.VMEM((4, 8, 64, 256), BF),
        pltpu.VMEM((4, 8, 64, 256), BF),
        pltpu.VMEM((EPAD, VPAD), F32),
        pltpu.VMEM((rows, 128), F32),
        pltpu.VMEM((8, VPAD), F32),
        pltpu.VMEM((2, 2, 2, 64, VPAD), F32),
        pltpu.VMEM((2, 2, 104, VPAD), F32),
        pltpu.VMEM((2, 64, VPAD), F32),
        pltpu.VMEM((64, VPAD), F32),
        pltpu.VMEM((2, 2, 2, EPAD, 256), F32),
        pltpu.VMEM((2, 104, 256), F32),
        pltpu.VMEM((112, 256), BF),
        pltpu.VMEM((112, 256), BF),
        pltpu.VMEM((64, VPAD), F32),
        pltpu.VMEM((3, 32, VPAD), F32),
        pltpu.VMEM((3, 32, VPAD), F32),
        pltpu.VMEM((3, 32, VPAD), F32),
        pltpu.VMEM((64, VPAD), F32),
        pltpu.VMEM((32, VPAD), F32),
        pltpu.VMEM((32, VPAD), F32),
    ]
    shapes = [
        (3,), (4,), (3, 2), (4, 2), (8, 2), (16, 2), (3,), (4,), (8,), (16,),
        (steps, 2, 3, 2), (n, 2), (steps, 2), (steps, 2, 3, 2), (3,), (4,), (11,), (10,), (6,), (3,),
    ]
    for shape in shapes:
        scratch += [dma(shape), dma(shape)]
    scratch += [dma((12,)), dma((steps, 2))]
    out_own, out_recv, out_in, out_dec, out_hid, out_small = pl.pallas_call(
        functools.partial(lstm_kernel, steps, rows),
        out_shape=(
            jax.ShapeDtypeStruct((8, own_rows, 256), F32),
            jax.ShapeDtypeStruct((3, 8, own_rows, 256), BF),
            jax.ShapeDtypeStruct((104, 256), F32),
            jax.ShapeDtypeStruct((own_rows, VPAD), F32),
            jax.ShapeDtypeStruct((micro * steps, count, width), BF),
            jax.ShapeDtypeStruct((EPAD, VPAD), F32),
        ),
        in_specs=[hbm] + [vm] * 8,
        out_specs=(vm, hbm, vm, vm, hbm, vm),
        scratch_shapes=scratch,
        compiler_params=pltpu.CompilerParams(
            collective_id=0, has_side_effects=True, vmem_limit_bytes=66 * 1000 * 1000
        ),
    )(
        w_rec, w_in, bias_in, w_dec, embed, bias_dec,
        chars.transpose(2, 0, 1), resets.transpose(2, 0, 1), targets.transpose(2, 0, 1),
    )
    everyone = lax.axis_size(("dp", "fsdp"))
    hid, table, g_in, g_bias, g_rec, g_dec, g_bias_dec, loss = pl.pallas_call(
        output_kernel,
        out_shape=(
            jax.ShapeDtypeStruct((micro * steps, count, width), BF),
            jax.ShapeDtypeStruct((vocab, emb), F32),
            jax.ShapeDtypeStruct((emb, 256), F32),
            jax.ShapeDtypeStruct((256,), F32),
            jax.ShapeDtypeStruct((own_rows, gate_cols), F32),
            jax.ShapeDtypeStruct((own_rows, vocab), F32),
            jax.ShapeDtypeStruct((vocab,), F32),
            jax.ShapeDtypeStruct((1, 1), F32),
        ),
        in_specs=[hbm, hbm, vm, vm, hbm, vm],
        out_specs=(hbm, vm, vm, vm, hbm, vm, vm, vm),
        scratch_shapes=[
            pltpu.VMEM((micro * steps, count, width), BF),
            pltpu.VMEM((8, own_rows, 256), F32),
            pltpu.VMEM((3, 8, own_rows, 256), BF),
            pltpu.VMEM((own_rows, gate_cols), F32),
            dma((12,)),
            dma((2,)),
        ],
    )(out_own, out_recv, out_in, out_dec, out_hid, out_small)
    return (
        loss[0, 0] / (micro * count * steps * everyone),
        hid.reshape(micro, steps, count, width).transpose(0, 2, 1, 3),
        table,
        g_in,
        g_bias,
        g_rec,
        g_dec,
        g_bias_dec,
    )


def dot_plain(left, right):
    return jnp.dot(left, right, preferred_element_type=jnp.float32)


def dot_right_t(left, right):
    return lax.dot_general(
        left, right, (((1,), (1,)), ((), ())), preferred_element_type=jnp.float32
    )


def dot_left_t(left, right):
    return lax.dot_general(
        left, right, (((0,), (0,)), ((), ())), preferred_element_type=jnp.float32
    )


def lstm_forward(weights, embed, bias_dec, ids, marks, goals):
    w_rec, w_dec, w_in, bias_in = weights
    count, steps = ids.shape
    width = w_rec.shape[0]
    letters = jnp.arange(embed.shape[0], dtype=jnp.int32)
    onehot = (ids.T.reshape(-1)[:, None] == letters[None, :]).astype(jnp.bfloat16)
    feature = dot_plain(onehot, embed).astype(jnp.bfloat16)
    drives = (dot_plain(feature, w_in) + bias_in.astype(jnp.float32)).reshape(steps, count, -1)
    keeps = (1 - marks.T).astype(jnp.float32)[:, :, None]

    def advance(state, slot):
        hidden_now, cell = state
        drive, keep_now = slot
        prev_hidden = hidden_now * keep_now.astype(jnp.bfloat16)
        prev_cell = cell * keep_now
        pre = drive + dot_plain(prev_hidden, w_rec)
        gin, gforget, gcand, gout = jnp.split(pre, 4, axis=1)
        cell_new = jax.nn.sigmoid(gforget) * prev_cell + jax.nn.sigmoid(gin) * jnp.tanh(gcand)
        hid_new = (jax.nn.sigmoid(gout) * jnp.tanh(cell_new)).astype(jnp.bfloat16)
        return ((hid_new, cell_new), (pre, prev_hidden, prev_cell, cell_new, hid_new))

    start = (jnp.zeros((count, width), jnp.bfloat16), jnp.zeros((count, width), jnp.float32))
    state, saved = lax.scan(advance, start, (drives, keeps))
    pres, prev_hiddens, prev_cells, cells, hiddens = saved
    flat_hidden = hiddens.reshape(steps * count, width)
    logits = dot_plain(flat_hidden, w_dec) + bias_dec.astype(jnp.float32)
    top = jnp.max(logits, axis=1, keepdims=True)
    shifted = jnp.exp(logits - top)
    summed = jnp.sum(shifted, axis=1, keepdims=True)
    goal_hot = (goals.T.reshape(-1)[:, None] == letters[None, :]).astype(jnp.float32)
    loss_part = jnp.sum(top[:, 0] + jnp.log(summed[:, 0])) - jnp.sum(goal_hot * logits)
    d_logits = (shifted / summed - goal_hot).astype(jnp.bfloat16)
    kept = (pres, prev_hiddens, prev_cells, cells, keeps, flat_hidden, d_logits, feature, onehot)
    return (kept, loss_part, jnp.transpose(hiddens, (1, 0, 2)))


def lstm_backward(weights, kept):
    w_rec, w_dec, w_in, bias_in = weights
    pres, prev_hiddens, prev_cells, cells, keeps, flat_hidden, d_logits, feature, onehot = kept
    steps, count, width = cells.shape
    from_dec = dot_right_t(d_logits, w_dec).reshape(steps, count, width)

    def retreat(carry, slot):
        grad_h, grad_c = carry
        pre, prev_cell, cell, extra, keep_now = slot
        gin, gforget, gcand, gout = jnp.split(pre, 4, axis=1)
        sig_in = jax.nn.sigmoid(gin)
        sig_forget = jax.nn.sigmoid(gforget)
        sig_out = jax.nn.sigmoid(gout)
        tan_cand = jnp.tanh(gcand)
        tan_cell = jnp.tanh(cell)
        grad_hid = extra + grad_h
        grad_out = grad_hid * tan_cell
        grad_cell = grad_c + grad_hid * sig_out * (1.0 - tan_cell * tan_cell)
        d_pre = jnp.concatenate(
            [
                grad_cell * tan_cand * sig_in * (1.0 - sig_in),
                grad_cell * prev_cell * sig_forget * (1.0 - sig_forget),
                grad_cell * sig_in * (1.0 - tan_cand * tan_cand),
                grad_out * sig_out * (1.0 - sig_out),
            ],
            axis=1,
        ).astype(jnp.bfloat16)
        back_h = dot_right_t(d_pre, w_rec) * keep_now
        back_c = grad_cell * sig_forget * keep_now
        return ((back_h, back_c), d_pre)

    start = (jnp.zeros((count, width), jnp.float32), jnp.zeros((count, width), jnp.float32))
    state, d_pres = lax.scan(
        retreat, start, (pres, prev_cells, cells, from_dec, keeps), reverse=True
    )
    flat_pre = d_pres.reshape(steps * count, -1)
    grad_dec = dot_left_t(flat_hidden, d_logits)
    grad_in = dot_left_t(feature, flat_pre)
    grad_bias = jnp.sum(flat_pre.astype(jnp.float32), axis=0)
    grad_feature = dot_right_t(flat_pre, w_in)
    grad_table = lax.dot_general(
        onehot.astype(jnp.float32),
        grad_feature,
        (((0,), (0,)), ((), ())),
        precision=lax.Precision.HIGHEST,
        preferred_element_type=jnp.float32,
    )
    grad_bias_out = jnp.sum(d_logits.astype(jnp.float32), axis=0)
    flat_prev = prev_hiddens.reshape(steps * count, width)
    return (grad_dec, grad_in, grad_bias, grad_table, grad_bias_out, flat_prev, flat_pre)


def general(chars, resets, targets, embed, w_in, bias_in, w_rec, w_dec, bias_dec):
    micro, count, steps = chars.shape
    everyone = lax.axis_size(("dp", "fsdp"))
    sums = None
    prev_list = []
    pre_list = []
    hidden_list = []
    for index in range(micro):
        forward_set = (
            lax.all_gather(w_rec, ("dp", "fsdp"), axis=0, tiled=True),
            lax.all_gather(w_dec, ("dp", "fsdp"), axis=0, tiled=True),
            lax.all_gather(w_in, ("dp", "fsdp"), axis=1, tiled=True),
            lax.all_gather(bias_in, ("dp", "fsdp"), axis=0, tiled=True),
        )
        kept, loss_part, hiddens = lstm_forward(
            forward_set, embed, bias_dec, chars[index], resets[index], targets[index]
        )
        backward_set = (
            lax.all_gather(w_rec, ("dp", "fsdp"), axis=0, tiled=True),
            lax.all_gather(w_dec, ("dp", "fsdp"), axis=0, tiled=True),
            lax.all_gather(w_in, ("dp", "fsdp"), axis=1, tiled=True),
            lax.all_gather(bias_in, ("dp", "fsdp"), axis=0, tiled=True),
        )
        grad_dec, grad_in, grad_bias, grad_table, grad_bias_out, flat_prev, flat_pre = (
            lstm_backward(backward_set, kept)
        )
        pieces = (grad_dec, grad_in, grad_bias, grad_table, grad_bias_out, loss_part)
        if sums is None:
            sums = pieces
        else:
            sums = tuple((first + second for first, second in zip(sums, pieces)))
        prev_list.append(flat_prev)
        pre_list.append(flat_pre)
        hidden_list.append(hiddens)
    prev_all = jnp.concatenate(prev_list, axis=0)
    pre_all = jnp.concatenate(pre_list, axis=0)
    grad_w_rec = lax.psum_scatter(
        dot_left_t(prev_all, pre_all), ("dp", "fsdp"), scatter_dimension=0, tiled=True
    )
    grad_w_dec, grad_w_in, grad_bias_in = (
        lax.psum_scatter(sums[0], ("dp", "fsdp"), scatter_dimension=0, tiled=True),
        lax.psum_scatter(sums[1], ("dp", "fsdp"), scatter_dimension=1, tiled=True),
        lax.psum_scatter(sums[2], ("dp", "fsdp"), scatter_dimension=0, tiled=True),
    )
    grad_embed, grad_bias_dec, total = lax.psum((sums[3], sums[4], sums[5]), ("dp", "fsdp"))
    loss = total / (micro * count * steps * everyone)
    hidden = jnp.stack(hidden_list, axis=0)
    return (
        loss,
        hidden,
        grad_embed,
        grad_w_in,
        grad_bias_in,
        grad_w_rec,
        grad_w_dec,
        grad_bias_dec,
    )


def solution(mesh):
    per_device = fused if (mesh.shape["dp"], mesh.shape["fsdp"]) == (8, 4) else general
    return jax.shard_map(
        per_device,
        mesh=mesh,
        in_specs=(
            P(None, ("dp", "fsdp"), None),
            P(None, ("dp", "fsdp"), None),
            P(None, ("dp", "fsdp"), None),
            P(),
            P(None, ("dp", "fsdp")),
            P(("dp", "fsdp")),
            P(("dp", "fsdp"), None),
            P(("dp", "fsdp"), None),
            P(),
        ),
        out_specs=(
            P(),
            P(None, ("dp", "fsdp"), None, None),
            P(),
            P(None, ("dp", "fsdp")),
            P(("dp", "fsdp")),
            P(("dp", "fsdp"), None),
            P(("dp", "fsdp"), None),
            P(),
        ),
        check_vma=False,
    )
```

profile of v0, /device:TPU:13, one launch (start us, length us, event | category | flops | bytes accessed | tf_op | source)
XLA Modules:
  0.0 253.7 jit_solution(10422114735954051700)
XLA Ops:
  0.6 246.1 %shard_map.152 = (f32[8,64,256]{2,1,0:T(8,128)}, bf16[3,8,64,256]{3,2,1,0:T(8,128)(2,1)}, f32[104,256]{1,0:T(8,128)}, f32[64,384]{1,0:T(8,128)}, bf16[12,32,2048]{2,1,0:T(8,128)(2,1)}, /*index=5*/f32[128,384]{1,0:T(8,128)}) custom-call(bf16[64,8192]{1,0:T(8,128)(2,1)} %w_rec.1, bf16[100,256]{1,0:T(8,128)(2,1)} %w_in_raw.1, bf16[256]{0:T(256)(128)(2,1)} %b_in_raw.1, ...), custom_call_target="tpu_custom_call" | custom-call | tf_op jit(solution)/shard_map/pallas_call | solution.py:1109
  246.7 5.2 %shard_map.153 = (bf16[12,32,2048]{2,1,0:T(8,128)(2,1)}, f32[275,100]{1,0:T(8,128)}, f32[100,256]{1,0:T(8,128)}, f32[256]{0:T(256)}, f32[64,8192]{1,0:T(8,128)},...) custom-call(f32[8,64,256]{2,1,0:T(8,128)} %get-tuple-element.22.own, ...), custom_call_target="tpu_custom_call" | custom-call | tf_op jit(solution)/shard_map/pallas_call | solution.py:1130
where the time goes:
time: 255 us; the launch traced here: 254 us
  Pallas kernels  251 us (98%)
    pallas_call x1, Pallas kernels, fused(): pl.pallas_call(functools.partial(lstm_kernel, steps, rows), out_shape=(ja...  246 us
    pallas_call x1, Pallas kernels, fused(): pl.pallas_call(output_kernel, out_shape=(jax.ShapeDtypeStruct((micro * st...  5.2 us

commit v1 on v0

--- a/solution.py
+++ b/solution.py
@@ -33,10 +33,10 @@
     w_rec, w_in_raw, b_in_raw, w_dec_raw, emb_raw, bias_raw, chars_in, resets_in, targets_in,
     out_own, out_recv, out_in, out_dec, out_hid, out_small,
     W, WIN, WDEC, IDS, H, HT, HTS, HSEND, A, C, D, DS, DRAW, DL,
-    ids_in, w_in, emb_t, w_dec, bias_dec, PR, STG, OWN, DCN, SY, RY, SM, RM, EMBT, LV, BD, GWD, GIS, GY, GM, DWI, IY, SIM, IM, RS1, RS2, RS3, RS4, RS5, PIECE, TOTAL,
+    ids_in, w_in, emb_t, w_dec, bias_dec, PR, STG, CB, PEND, OWN, DCN, SY, RY, SM, RM, EMBT, LV, BD, GWD, GIS, GY, GM, DWI, SIY, IY, SIM, IM, RS1, RS2, RS3, RS4, RS5, PIECE, TOTAL,
     s_ids, r_ids, s_win, r_win, s_wa, r_wa, s_wm, r_wm, s_wy, r_wy, s_ws, r_ws,
     s_da, r_da, s_dm, r_dm, s_dy, r_dy, s_ds, r_ds, s_h, r_h, s_ht, r_ht, s_d, r_d,
-    s_pr, r_pr, s_gd, r_gd, s_gi, r_gi, s_sm, r_sm, s_ry, r_ry, s_rm, r_rm, s_ra, r_ra,
+    s_pr, r_pr, s_ph, r_ph, s_cb, r_cb, s_gd, r_gd, s_gi, r_gi, s_sm, r_sm, s_ry, r_ry, s_rm, r_rm, s_ra, r_ra,
     l_sem, hid_sem,
 ):
     last = steps - 1
@@ -513,6 +513,7 @@
             def _(n):
                 aside(n // 2, n % 2)
 
+
     def pr_copy(t, s, k, j):
         return rc(STG.at[s, k - 1, j], PR.at[t % 2, s, k - 1, j], s_pr.at[t, s, k - 1, j], r_pr.at[t, s, k - 1, j], kdev(k))
 
@@ -521,22 +522,17 @@
 
     def turn():
         def rows_of(q):
-            return pl.ds(pl.multiple_of(256 * q, 256), 256)
+            return slice(256 * q, 256 * (q + 1))
 
         def swap(p, q):
             upper, lower = W[p, rows_of(q), :].T, W[q, rows_of(p), :].T
             W[p, rows_of(q), :] = lower
             W[q, rows_of(p), :] = upper
 
-        @pl.loop(0, 8)
-        def _(p):
+        for p in range(8):
             W[p, rows_of(p), :] = W[p, rows_of(p), :].T
-            for step in (1, 2, 3):
-                swap(p, (p + step) % 8)
-
-        @pl.loop(0, 4)
-        def _(p):
-            swap(p, p + 4)
+            for q in range(p):
+                swap(p, q)
 
     def cell_back(t, s, oldest):
         keep = keep_of(t, s)
@@ -544,7 +540,8 @@
             up = WDEC[span(0, j), :]
             dh = mm(DL[t, s], up, NT)
             rest = PR[(t + 1) % 2, s, 0, j].astype(F32) + PR[(t + 1) % 2, s, 1, j].astype(F32)
-            rest = rest + PR[(t + 1) % 2, s, 2, j].astype(F32)
+            if j == 1:
+                rest = rest + PR[(t + 1) % 2, s, 2, j].astype(F32)
             dh = dh + (OWN[s, j] + rest)
             s_i, s_f, t_g, s_o = (A[t, s, 4 * j + g] for g in range(4))
             t_c = jnp.tanh(C[t, s, j])
@@ -564,21 +561,56 @@
                 if not oldest:
                     D[4 * j + g, t - 1, s] = low * keep.astype(BF)
 
-    def pr_each(act):
-        for k in (3, 1, 2):
-            for j in (0, 1):
-                act(k, j)
+    def part_rows(h):
+        return slice(64 * h, 64 * (h + 1))
+
+    def pr_half(t, s, k, h):
+        src, dst = STG.at[s, k - 1, 0, part_rows(h)], PR.at[t % 2, s, k - 1, 0, part_rows(h)]
+        return rc(src, dst, s_ph.at[t, s, k - 1, h], r_ph.at[t, s, k - 1, h], kdev(k))
+
+    def owed_copy(t, s, n):
+        return rc(STG.at[s, 2, 0, part_rows(n)], CB.at[s, n], s_cb.at[t, s, n], r_cb.at[t, s, n], kdev(1 + n))
+
+    def pr_arrived(t, s):
+        for k in (1, 2, 3):
+            pr_copy(t, s, k, 1).wait_recv()
+        for k in (1, 2):
+            for h in (0, 1):
+                pr_half(t, s, k, h).wait_recv()
+
+    def pr_left(t, s):
+        for k in (1, 2, 3):
+            pr_copy(t, s, k, 1).wait_send()
+        for k in (1, 2):
+            for h in (0, 1):
+                pr_half(t, s, k, h).wait_send()
+        for n in (0, 1):
+            owed_copy(t, s, n).wait_send()
 
     def product_back(t, s):
         left = jnp.concatenate([D[q, t - 1, s] for q in range(8)], axis=1)
-        for k in (3, 1, 2, 0):
-            for j in (0, 1):
-                total = mm(left, W[2 * k + j], NN)
-                if k == 0:
-                    OWN[s, j] = total
-                else:
-                    STG[s, k - 1, j] = total.astype(BF)
-        pr_each(lambda k, j: pr_copy(t, s, k, j).start())
+        for k, j in ((3, 0), (3, 1), (1, 0), (1, 1), (2, 0), (2, 1), (0, 0), (0, 1)):
+            total = mm(left, W[2 * k + j], NN)
+            if k == 0:
+                OWN[s, j] = total
+                continue
+            STG[s, k - 1, j] = total.astype(BF)
+            if k == 3 and j == 0:
+                owed_copy(t, s, 0).start()
+                owed_copy(t, s, 1).start()
+            elif j == 0:
+                PEND[k - 1] = total[part_rows(2 - k)]
+        pr_copy(t, s, 3, 1).start()
+        for k in (1, 2):
+            pr_half(t, s, k, k - 1).start()
+            pr_copy(t, s, k, 1).start()
+
+    def add_owed(t, s):
+        for k in (2, 1):
+            h = 2 - k
+            owed_copy(t, s, h).wait_recv()
+            STG[s, k - 1, 0, part_rows(h)] = (PEND[k - 1] + CB[s, h].astype(F32)).astype(BF)
+            pr_half(t, s, k, h).start()
 
     def input_side(t, s):
         onehot = letter(t, s)
@@ -602,38 +634,46 @@
     def gd_m():
         return rc(GWD.at[1 - zh, y, c], GM, s_gd.at[2], r_gd.at[2], mir)
 
+    turn()
+
     @pl.loop(0, 2 * (steps - 1))
     def _(i):
         t, s = last - i // 2, i % 2
 
         @pl.when(i < 2)
         def _():
-            wait_h(last, s)
+            wait_h(t, s)
             logits_of(last, s)
 
         @pl.when(i >= 2)
         def _():
-            pr_each(lambda k, j: pr_copy(t + 1, s, k, j).wait_recv())
+            pr_arrived(t + 1, s)
 
         cell_back(t, s, False)
+
+        @pl.when(i >= 1)
+        def _():
+            add_owed(t + 1 - s, 1 - s)
+
         d_copy(t, s).start()
 
         @pl.when(i >= 2)
         def _():
-            pr_each(lambda k, j: pr_copy(t + 1, s, k, j).wait_send())
-
-        @pl.when(i == 0)
-        def _():
-            turn()
+            pr_left(t + 1, s)
 
         product_back(t, s)
         input_side(t, s)
 
         @pl.when(i < 2)
         def _():
-            aside(last - 1, s)
-
-        @pl.when(i == 3)
+            logits_of(last - 1, s)
+
+        @pl.when(jnp.logical_and(i >= 2, i < 4))
+        def _():
+            decoder_side(last - 1, s)
+            transposed_side(last - 1, s)
+
+        @pl.when(i == 4)
         def _():
             @pl.loop(0, 2)
             def _(n):
@@ -641,19 +681,19 @@
 
             gd_s().start()
 
-        @pl.when(i == 4)
+        @pl.when(i == 5)
         def _():
             gd_s().wait_recv()
             GWD[:, :, c] += GIS[:, :, 0:64]
             gd_y().start()
 
-        @pl.when(i == 6)
+        @pl.when(i == 7)
         def _():
             gd_y().wait_recv()
             GWD[:, y, c] += GY[...]
             gd_m().start()
 
-        @pl.when(i == 8)
+        @pl.when(i == 9)
         def _():
             gd_m().wait_recv()
             out_dec[...] = GWD[zh, y, c] + GM[...]
@@ -740,11 +780,8 @@
 
     def pass_on(k):
         if k == 3:
-            hold = kept(k)
             for h in (0, 1):
-                ry_half(h).wait_recv()
-                SM[3, half(h)] = (hold[half(h)] + RY[3, half(h)].astype(F32)).astype(BF)
-                rm_half(h).start()
+                pass_half(h)
             return
         add_y(k)
         SM[k] = kept(k)[...].astype(BF)
@@ -853,20 +890,29 @@
         return rc(DWI.at[:, :, 1 - c, live], GIS.at[:, :, :, 0:256], s_gi.at[0], r_gi.at[0], sib)
 
     def gi_y():
-        return rc(DWI.at[:, 1 - y, c, live], IY, s_gi.at[1], r_gi.at[1], ydev)
+        return rc(SIY, IY, s_gi.at[1], r_gi.at[1], ydev)
 
     def gi_m():
         return rc(SIM, IM, s_gi.at[2], r_gi.at[2], mir)
 
     def gi_p():
         return rc(DWI.at[zh, y, c, live], out_in, s_gi.at[3], r_gi.at[3], back)
+
+    def pass_half(h):
+        ry_half(h).wait_recv()
+        SM[3, half(h)] = (kept(3)[half(h)] + RY[3, half(h)].astype(F32)).astype(BF)
+        rm_half(h).start()
 
     def first_position():
         @pl.loop(0, 2)
         def _(s):
-            pr_each(lambda k, j: pr_copy(1, s, k, j).wait_recv())
+            pr_arrived(1, s)
             cell_back(0, s, True)
             input_side(0, s)
+
+            @pl.when(jnp.logical_and(inner, s == 0))
+            def _():
+                pass_half(0)
 
         leader = jnp.logical_and(x == 0, a == 0)
         high_row = lax.broadcasted_iota(jnp.int32, (8, VPAD), 0)
@@ -882,16 +928,22 @@
     def _(p):
         make_tile(p)
 
+        @pl.when(p == 0)
+        def _():
+            add_owed(1, 1)
+
         @pl.when(p == 1)
         def _():
+            first_position()
+            sm_step1()
             @pl.when(inner)
             def _():
-                settle(0)
-
-            first_position()
-            sm_step1()
+                pass_half(1)
+
             gi_s().wait_recv()
             DWI[:, :, c, 0:104] = DWI[:, :, c, 0:104] + GIS[:, :, :, 0:256]
+            sm_step2()
+            SIY[...] = DWI[:, 1 - y, c, 0:112].astype(BF)
             gi_y().start()
 
             @pl.when(outer)
@@ -905,23 +957,23 @@
         @pl.when(p == 3)
         def _():
             gi_y().wait_recv()
-            DWI[:, y, c, 0:104] = DWI[:, y, c, 0:104] + IY[...]
+            DWI[:, y, c, 0:104] = DWI[:, y, c, 0:104] + IY[...].astype(F32)[:, 0:104]
             SIM[...] = DWI[1 - zh, y, c, 0:112].astype(BF)
             gi_m().start()
 
         @pl.when(p == 4)
         def _():
             settle(2)
+            sm_step3()
 
         @pl.when(p == 5)
         def _():
             settle(3)
 
-    sm_step2()
     settle(4)
     settle(5)
+    sm_step4()
     settle(6)
-    sm_step3()
     gi_m().wait_recv()
     DWI[zh, y, c, 0:104] = DWI[zh, y, c, 0:104] + IM[...].astype(F32)[0:104]
 
@@ -933,15 +985,12 @@
     def _():
         out_in[...] = DWI[zh, y, c, 0:104]
 
-    sm_step4()
+    sm_step5()
     settle(7)
-    sm_step5()
 
     for k in (1, 2, 3):
         for j in (0, 1):
             wa(k, j).wait_send()
-            for s in range(2):
-                pr_copy(1, s, k, j).wait_send()
         ids_copy(k, member(0)).wait_send()
         da(k).wait_send()
         ra_copy(k).wait()
@@ -952,6 +1001,8 @@
         gi_p().wait()
         win_perm(x, z // 2, z % 2).wait_send()
 
+    for s in range(2):
+        pr_left(1, s)
     win_mir(zh).wait_send()
     win_y(y).wait_send()
     win_s(c).wait_send()
@@ -992,53 +1043,57 @@
 
 def output_kernel(
     own, recv, g_in, g_dec, hid_in, small, hid, table, o_in, o_bias, o_rec, o_dec, o_bias_dec, loss,
-    h_buf, own_buf, recv_buf, rec_buf, in_sem, out_sem,
+    h_buf, own_buf, recv_buf, rec_buf, in_buf, dec_buf, small_buf, t_buf, i_buf, b_buf, d_buf, bd_buf, l_buf, in_sem, out_sem,
 ):
     dp = lax.axis_index("dp")
     z, x = dp // 2, dp % 2
     a = z + (z // 2) * (3 - 2 * z)
-    parts = 8
 
     def cols(k, j, g):
         xk, ak = x + (k % 2) * (1 - 2 * x), a + (k // 2) * (1 - 2 * a)
         ub = 2 * (ak + j * (3 - 2 * ak)) + xk
         return pl.ds(pl.multiple_of(256 * (8 * g + ub), 256), 256)
 
-    def hid_load(p):
-        return pltpu.make_async_copy(hid_in.at[:, :, 256 * p : 256 * (p + 1)], h_buf.at[:, :, cols(p // 2, p % 2, 0)], in_sem.at[p])
-
-    def hid_store():
-        return pltpu.make_async_copy(h_buf, hid, out_sem.at[1])
-
-    def rec_load(k):
-        if k == 0:
-            return pltpu.make_async_copy(own, own_buf, in_sem.at[parts])
-        return pltpu.make_async_copy(recv.at[k - 1], recv_buf.at[k - 1], in_sem.at[parts + k])
-
-    for p in range(parts):
-        hid_load(p).start()
+    def load(n, src, dst):
+        copy = pltpu.make_async_copy(src, dst, in_sem.at[n])
+        copy.start()
+        return copy
+
+    def store(n, src, dst):
+        copy = pltpu.make_async_copy(src, dst, out_sem.at[n])
+        copy.start()
+        return copy
+
+    hid_loads = [
+        load(p, hid_in.at[:, :, 256 * p : 256 * (p + 1)], h_buf.at[:, :, cols(p // 2, p % 2, 0)]) for p in range(8)
+    ]
+    rec_loads = [load(8, own, own_buf), load(9, recv, recv_buf)]
+    small_loads = [load(10, small, small_buf), load(11, g_in, in_buf), load(12, g_dec, dec_buf)]
+    for copy in hid_loads:
+        copy.wait()
+    stores = [store(0, h_buf, hid)]
+    for copy in rec_loads:
+        copy.wait()
     for k in range(4):
-        rec_load(k).start()
-    for p in range(parts):
-        hid_load(p).wait()
-    hid_store().start()
-    vocab, emb = table.shape
-    table[...] = small[0:SMALL, :].T[:vocab, :emb]
-    o_in[...] = g_in[0:emb, :]
-    o_bias[...] = g_in[emb, :]
-    o_dec[...] = g_dec[:, :vocab]
-    o_bias_dec[...] = small[SMALL - 8, :vocab]
-    loss[...] = small[SMALL - 7 : SMALL - 6, 0:1]
-    for k in range(4):
-        rec_load(k).wait()
         for j in (0, 1):
             for g in range(4):
                 part = own_buf[4 * j + g] if k == 0 else recv_buf[k - 1, 4 * j + g].astype(F32)
                 rec_buf[:, cols(k, j, g)] = part
-    rec_store = pltpu.make_async_copy(rec_buf, o_rec, out_sem.at[0])
-    rec_store.start()
-    rec_store.wait()
-    hid_store().wait()
+    stores.append(store(1, rec_buf, o_rec))
+    for copy in small_loads:
+        copy.wait()
+    vocab, emb = table.shape
+    t_buf[...] = small_buf[0:SMALL, :].T[:vocab, :emb]
+    i_buf[...] = in_buf[0:emb, :]
+    b_buf[...] = in_buf[emb, :]
+    d_buf[...] = dec_buf[:, :vocab]
+    bd_buf[...] = small_buf[SMALL - 8, :vocab]
+    l_buf[...] = small_buf[SMALL - 7 : SMALL - 6, 0:1]
+    pairs = ((t_buf, table), (i_buf, o_in), (b_buf, o_bias), (d_buf, o_dec), (bd_buf, o_bias_dec), (l_buf, loss))
+    for n, (src, dst) in enumerate(pairs):
+        stores.append(store(2 + n, src, dst))
+    for copy in stores:
+        copy.wait()
 
 
 def fused(chars, resets, targets, embed, w_in, bias_in, w_rec, w_dec, bias_dec):
@@ -1074,6 +1129,8 @@
         pltpu.VMEM((8, VPAD), F32),
         pltpu.VMEM((2, micro, 3, 2, rows, 256), BF),
         pltpu.VMEM((micro, 3, 2, rows, 256), BF),
+        pltpu.VMEM((micro, 2, rows // 2, 256), BF),
+        pltpu.VMEM((2, rows // 2, 256), F32),
         pltpu.VMEM((micro, 2, rows, 256), F32),
         pltpu.VMEM((micro, 2, rows, 256), F32),
         pltpu.VMEM((4, 8, 64, 256), BF),
@@ -1088,7 +1145,8 @@
         pltpu.VMEM((2, 64, VPAD), F32),
         pltpu.VMEM((64, VPAD), F32),
         pltpu.VMEM((2, 2, 2, EPAD, 256), F32),
-        pltpu.VMEM((2, 104, 256), F32),
+        pltpu.VMEM((2, 112, 256), BF),
+        pltpu.VMEM((2, 112, 256), BF),
         pltpu.VMEM((112, 256), BF),
         pltpu.VMEM((112, 256), BF),
         pltpu.VMEM((64, VPAD), F32),
@@ -1101,7 +1159,8 @@
     ]
     shapes = [
         (3,), (4,), (3, 2), (4, 2), (8, 2), (16, 2), (3,), (4,), (8,), (16,),
-        (steps, 2, 3, 2), (n, 2), (steps, 2), (steps, 2, 3, 2), (3,), (4,), (11,), (10,), (6,), (3,),
+        (steps, 2, 3, 2), (n, 2), (steps, 2), (steps, 2, 3, 2),
+        (steps, 2, 2, 2), (steps, 2, 2), (3,), (4,), (11,), (10,), (6,), (3,),
     ]
     for shape in shapes:
         scratch += [dma(shape), dma(shape)]
@@ -1139,15 +1198,24 @@
             jax.ShapeDtypeStruct((vocab,), F32),
             jax.ShapeDtypeStruct((1, 1), F32),
         ),
-        in_specs=[hbm, hbm, vm, vm, hbm, vm],
-        out_specs=(hbm, vm, vm, vm, hbm, vm, vm, vm),
+        in_specs=[hbm] * 6,
+        out_specs=(hbm,) * 8,
         scratch_shapes=[
             pltpu.VMEM((micro * steps, count, width), BF),
             pltpu.VMEM((8, own_rows, 256), F32),
             pltpu.VMEM((3, 8, own_rows, 256), BF),
             pltpu.VMEM((own_rows, gate_cols), F32),
-            dma((12,)),
-            dma((2,)),
+            pltpu.VMEM((104, 256), F32),
+            pltpu.VMEM((own_rows, VPAD), F32),
+            pltpu.VMEM((EPAD, VPAD), F32),
+            pltpu.VMEM((vocab, emb), F32),
+            pltpu.VMEM((emb, 256), F32),
+            pltpu.VMEM((256,), F32),
+            pltpu.VMEM((own_rows, vocab), F32),
+            pltpu.VMEM((vocab,), F32),
+            pltpu.VMEM((1, 1), F32),
+            dma((13,)),
+            dma((8,)),
         ],
     )(out_own, out_recv, out_in, out_dec, out_hid, out_small)
     return (

time: 255 us -> 248 us (0.973)
  Pallas kernels: 251 us -> 243 us
    pallas_call x1, Pallas kernels: 246 us -> 239 us  [fused(): pl.pallas_call(functools.partial(lstm_kernel, steps, rows), out_shape=(ja...]
where the time goes in v1:
time: 248 us; the launch traced here: 245 us
  Pallas kernels  243 us (98%)
    pallas_call x1, Pallas kernels, fused(): pl.pallas_call(functools.partial(lstm_kernel, steps, rows), out_shape=(ja...  239 us

profile of v1, /device:TPU:13, one launch (start us, length us, event | category | flops | bytes accessed | tf_op | source)
XLA Modules:
  0.0 245.1 jit_solution(5823231806747359686)
XLA Ops:
  0.6 239.0 %shard_map.152 = (f32[8,64,256]{2,1,0:T(8,128)}, bf16[3,8,64,256]{3,2,1,0:T(8,128)(2,1)}, f32[104,256]{1,0:T(8,128)}, f32[64,384]{1,0:T(8,128)}, bf16[12,32,2048]{2,1,0:T(8,128)(2,1)}, /*index=5*/f32[128,384]{1,0:T(8,128)}) custom-call(bf16[64,8192]{1,0:T(8,128)(2,1)} %w_rec.1, bf16[100,256]{1,0:T(8,128)(2,1)} %w_in_raw.1, bf16[256]{0:T(256)(128)(2,1)} %b_in_raw.1, ...), custom_call_target="tpu_custom_call" | custom-call | tf_op jit(solution)/shard_map/pallas_call | solution.py:1168
  239.6 3.7 %shard_map.153 = (bf16[12,32,2048]{2,1,0:T(8,128)(2,1)}, f32[275,100]{1,0:T(8,128)}, f32[100,256]{1,0:T(8,128)}, f32[256]{0:T(256)}, f32[64,8192]{1,0:T(8,128)},...) custom-call(f32[8,64,256]{2,1,0:T(8,128)} %get-tuple-element.22.own, ...), custom_call_target="tpu_custom_call" | custom-call | tf_op jit(solution)/shard_map/pallas_call | solution.py:1189

commit v2 on v1

--- a/solution.py
+++ b/solution.py
@@ -33,10 +33,10 @@
     w_rec, w_in_raw, b_in_raw, w_dec_raw, emb_raw, bias_raw, chars_in, resets_in, targets_in,
     out_own, out_recv, out_in, out_dec, out_hid, out_small,
     W, WIN, WDEC, IDS, H, HT, HTS, HSEND, A, C, D, DS, DRAW, DL,
-    ids_in, w_in, emb_t, w_dec, bias_dec, PR, STG, CB, PEND, OWN, DCN, SY, RY, SM, RM, EMBT, LV, BD, GWD, GIS, GY, GM, DWI, SIY, IY, SIM, IM, RS1, RS2, RS3, RS4, RS5, PIECE, TOTAL,
+    ids_in, w_in, emb_t, w_dec, bias_dec, PR, STG, CB, PEND, OWN, DCN, SY, RY, SM, RM, EMBT, LV, BD, GWD, GIS, GY, GM, DWI, SIY, IY, SIM, IM, RS1, RS2, RS3, RS4, RS5, PIECE, PAIR, TOTAL,
     s_ids, r_ids, s_win, r_win, s_wa, r_wa, s_wm, r_wm, s_wy, r_wy, s_ws, r_ws,
     s_da, r_da, s_dm, r_dm, s_dy, r_dy, s_ds, r_ds, s_h, r_h, s_ht, r_ht, s_d, r_d,
-    s_pr, r_pr, s_ph, r_ph, s_cb, r_cb, s_gd, r_gd, s_gi, r_gi, s_sm, r_sm, s_ry, r_ry, s_rm, r_rm, s_ra, r_ra,
+    s_ph, r_ph, s_cb, r_cb, s_gd, r_gd, s_gi, r_gi, s_sm, r_sm, s_ry, r_ry, s_rm, r_rm, s_ra, r_ra,
     l_sem, hid_sem,
 ):
     last = steps - 1
@@ -76,9 +76,9 @@
         return slice(256 * (2 * k + j), 256 * (2 * k + j + 1))
 
     mir, ydev, sib = dev(3 - z, x, y, c), dev(z, x, 1 - y, c), dev(z, x, y, 1 - c)
-    cross = dev(3 - z, x, 1 - y, c)
-    perm = dev(2 * x + y, c, z // 2, z % 2)
-    back = dev(2 * y + c, z // 2, z % 2, x)
+    side = x + y - 2 * x * y
+    perm = dev(side + zh * (3 - 2 * side), c, x, z % 2)
+    back = dev(2 * zh + c, y, a + y - 2 * a * y, x)
     stays = jnp.logical_and(perm[0] == dp, perm[1] == fs)
     moved = jnp.logical_not(stays)
 
@@ -109,7 +109,7 @@
 
     for k in (1, 2, 3):
         greet(kdev(k))
-    for to in (mir, ydev, sib, cross):
+    for to in (mir, ydev, sib):
         greet(to)
 
     @pl.when(moved)
@@ -117,7 +117,7 @@
         greet(perm)
         greet(back)
 
-    pl.semaphore_wait(barrier, 7 + 2 * moved.astype(jnp.int32))
+    pl.semaphore_wait(barrier, 6 + 2 * moved.astype(jnp.int32))
 
 
     def d_slot(b):
@@ -213,17 +213,17 @@
         to_s(0, j).start()
 
     def win_mir(jj):
-        return rc(WIN.at[jj, y, c], WIN.at[jj, y, c], s_win.at[1], r_win.at[1], mir)
+        return rc(WIN.at[y, jj, c], WIN.at[y, jj, c], s_win.at[1], r_win.at[1], mir)
 
     def win_y(yy):
-        return rc(WIN.at[:, yy, c], WIN.at[:, yy, c], s_win.at[2], r_win.at[2], ydev)
+        return rc(WIN.at[yy, :, c], WIN.at[yy, :, c], s_win.at[2], r_win.at[2], ydev)
 
     def win_s(cc):
         return rc(WIN.at[:, :, cc], WIN.at[:, :, cc], s_win.at[3], r_win.at[3], sib)
 
     @pl.when(moved)
     def _():
-        win_perm(zh, y, c).wait_recv()
+        win_perm(y, zh, c).wait_recv()
 
     @pl.when(stays)
     def _():
@@ -514,9 +514,6 @@
                 aside(n // 2, n % 2)
 
 
-    def pr_copy(t, s, k, j):
-        return rc(STG.at[s, k - 1, j], PR.at[t % 2, s, k - 1, j], s_pr.at[t, s, k - 1, j], r_pr.at[t, s, k - 1, j], kdev(k))
-
     def d_copy(t, s):
         return rc(D.at[:, t - 1, s], DS.at[:, t - 1, s], s_d.at[t, s], r_d.at[t, s], sib)
 
@@ -540,8 +537,6 @@
             up = WDEC[span(0, j), :]
             dh = mm(DL[t, s], up, NT)
             rest = PR[(t + 1) % 2, s, 0, j].astype(F32) + PR[(t + 1) % 2, s, 1, j].astype(F32)
-            if j == 1:
-                rest = rest + PR[(t + 1) % 2, s, 2, j].astype(F32)
             dh = dh + (OWN[s, j] + rest)
             s_i, s_f, t_g, s_o = (A[t, s, 4 * j + g] for g in range(4))
             t_c = jnp.tanh(C[t, s, j])
@@ -565,25 +560,22 @@
         return slice(64 * h, 64 * (h + 1))
 
     def pr_half(t, s, k, h):
-        src, dst = STG.at[s, k - 1, 0, part_rows(h)], PR.at[t % 2, s, k - 1, 0, part_rows(h)]
+        src, dst = STG.at[s, k - 1, :, part_rows(h)], PR.at[t % 2, s, k - 1, :, part_rows(h)]
         return rc(src, dst, s_ph.at[t, s, k - 1, h], r_ph.at[t, s, k - 1, h], kdev(k))
 
     def owed_copy(t, s, n):
-        return rc(STG.at[s, 2, 0, part_rows(n)], CB.at[s, n], s_cb.at[t, s, n], r_cb.at[t, s, n], kdev(1 + n))
-
-    def pr_arrived(t, s):
-        for k in (1, 2, 3):
-            pr_copy(t, s, k, 1).wait_recv()
+        return rc(STG.at[s, 2, :, part_rows(n)], CB.at[s, n], s_cb.at[t, s, n], r_cb.at[t, s, n], kdev(1 + n))
+
+    def pr_each(act):
         for k in (1, 2):
             for h in (0, 1):
-                pr_half(t, s, k, h).wait_recv()
+                act(k, h)
+
+    def pr_arrived(t, s):
+        pr_each(lambda k, h: pr_half(t, s, k, h).wait_recv())
 
     def pr_left(t, s):
-        for k in (1, 2, 3):
-            pr_copy(t, s, k, 1).wait_send()
-        for k in (1, 2):
-            for h in (0, 1):
-                pr_half(t, s, k, h).wait_send()
+        pr_each(lambda k, h: pr_half(t, s, k, h).wait_send())
         for n in (0, 1):
             owed_copy(t, s, n).wait_send()
 
@@ -595,21 +587,19 @@
                 OWN[s, j] = total
                 continue
             STG[s, k - 1, j] = total.astype(BF)
-            if k == 3 and j == 0:
+            if k < 3:
+                PEND[k - 1, j] = total[part_rows(2 - k)]
+            elif j == 1:
                 owed_copy(t, s, 0).start()
                 owed_copy(t, s, 1).start()
-            elif j == 0:
-                PEND[k - 1] = total[part_rows(2 - k)]
-        pr_copy(t, s, 3, 1).start()
         for k in (1, 2):
             pr_half(t, s, k, k - 1).start()
-            pr_copy(t, s, k, 1).start()
 
     def add_owed(t, s):
         for k in (2, 1):
             h = 2 - k
             owed_copy(t, s, h).wait_recv()
-            STG[s, k - 1, 0, part_rows(h)] = (PEND[k - 1] + CB[s, h].astype(F32)).astype(BF)
+            STG[s, k - 1, :, part_rows(h)] = (PEND[k - 1] + CB[s, h].astype(F32)).astype(BF)
             pr_half(t, s, k, h).start()
 
     def input_side(t, s):
@@ -662,7 +652,10 @@
             pr_left(t + 1, s)
 
         product_back(t, s)
-        input_side(t, s)
+
+        @pl.when(i < 2 * (steps - 1) - 1)
+        def _():
+            input_side(t, s)
 
         @pl.when(i < 2)
         def _():
@@ -822,7 +815,7 @@
         return rc(out_small.at[piece_rows(xx)], RS2.at[k - 1], s_sm.at[k], r_sm.at[k], kdev(k))
 
     def sm_quarter(n):
-        return rc(PIECE, RS3.at[n], s_sm.at[4 + n], r_sm.at[4 + n], (ydev, mir, cross)[n])
+        return rc(PIECE if n == 0 else PAIR, RS3.at[n], s_sm.at[4 + n], r_sm.at[4 + n], (ydev, mir)[n])
 
     def sm_spread(k):
         return rc(TOTAL, RS4.at[k - 1], s_sm.at[6 + k], r_sm.at[6 + k], kdev(k))
@@ -849,15 +842,20 @@
             for k in (1, 2, 3):
                 sm_group(k).wait_recv()
             PIECE[...] = (out_small[piece_rows(x)] + RS2[0]) + (RS2[1] + RS2[2])
-            for n in range(3):
-                sm_quarter(n).start()
+            sm_quarter(0).start()
+
+    def sm_step_mir():
+        @pl.when(outer)
+        def _():
+            sm_quarter(0).wait_recv()
+            PAIR[...] = PIECE[...] + RS3[0]
+            sm_quarter(1).start()
 
     def sm_step3():
         @pl.when(outer)
         def _():
-            for n in range(3):
-                sm_quarter(n).wait_recv()
-            TOTAL[...] = (PIECE[...] + RS3[0]) + (RS3[1] + RS3[2])
+            sm_quarter(1).wait_recv()
+            TOTAL[...] = PAIR[...] + RS3[1]
             for k in (1, 2, 3):
                 sm_spread(k).start()
 
@@ -896,7 +894,7 @@
         return rc(SIM, IM, s_gi.at[2], r_gi.at[2], mir)
 
     def gi_p():
-        return rc(DWI.at[zh, y, c, live], out_in, s_gi.at[3], r_gi.at[3], back)
+        return rc(DWI.at[y, zh, c, live], out_in, s_gi.at[3], r_gi.at[3], back)
 
     def pass_half(h):
         ry_half(h).wait_recv()
@@ -934,16 +932,18 @@
 
         @pl.when(p == 1)
         def _():
+            input_side(1, 1)
             first_position()
             sm_step1()
             @pl.when(inner)
             def _():
                 pass_half(1)
+                settle(1)
 
             gi_s().wait_recv()
             DWI[:, :, c, 0:104] = DWI[:, :, c, 0:104] + GIS[:, :, :, 0:256]
             sm_step2()
-            SIY[...] = DWI[:, 1 - y, c, 0:112].astype(BF)
+            SIY[...] = DWI[1 - y, :, c, 0:112].astype(BF)
             gi_y().start()
 
             @pl.when(outer)
@@ -952,13 +952,17 @@
 
         @pl.when(p == 2)
         def _():
-            settle(1)
+            @pl.when(outer)
+            def _():
+                settle(1)
+
+            sm_step_mir()
 
         @pl.when(p == 3)
         def _():
             gi_y().wait_recv()
-            DWI[:, y, c, 0:104] = DWI[:, y, c, 0:104] + IY[...].astype(F32)[:, 0:104]
-            SIM[...] = DWI[1 - zh, y, c, 0:112].astype(BF)
+            DWI[y, :, c, 0:104] = DWI[y, :, c, 0:104] + IY[...].astype(F32)[:, 0:104]
+            SIM[...] = DWI[y, 1 - zh, c, 0:112].astype(BF)
             gi_m().start()
 
         @pl.when(p == 4)
@@ -975,7 +979,7 @@
     sm_step4()
     settle(6)
     gi_m().wait_recv()
-    DWI[zh, y, c, 0:104] = DWI[zh, y, c, 0:104] + IM[...].astype(F32)[0:104]
+    DWI[y, zh, c, 0:104] = DWI[y, zh, c, 0:104] + IM[...].astype(F32)[0:104]
 
     @pl.when(moved)
     def _():
@@ -983,7 +987,7 @@
 
     @pl.when(stays)
     def _():
-        out_in[...] = DWI[zh, y, c, 0:104]
+        out_in[...] = DWI[y, zh, c, 0:104]
 
     sm_step5()
     settle(7)
@@ -1008,8 +1012,9 @@
     win_s(c).wait_send()
     @pl.when(outer)
     def _():
+        sm_quarter(0).wait_send()
+        sm_quarter(1).wait_send()
         for k in (1, 2, 3):
-            sm_quarter(k - 1).wait_send()
             sm_spread(k).wait_send()
 
     for copy in (gd_s, gd_y, gd_m, gi_s, gi_y, gi_m, sm_last):
@@ -1127,10 +1132,10 @@
         pltpu.VMEM((EPAD, VPAD), BF),
         pltpu.VMEM((own_rows, VPAD), BF),
         pltpu.VMEM((8, VPAD), F32),
-        pltpu.VMEM((2, micro, 3, 2, rows, 256), BF),
+        pltpu.VMEM((2, micro, 2, 2, rows, 256), BF),
         pltpu.VMEM((micro, 3, 2, rows, 256), BF),
-        pltpu.VMEM((micro, 2, rows // 2, 256), BF),
-        pltpu.VMEM((2, rows // 2, 256), F32),
+        pltpu.VMEM((micro, 2, 2, rows // 2, 256), BF),
+        pltpu.VMEM((2, 2, rows // 2, 256), F32),
         pltpu.VMEM((micro, 2, rows, 256), F32),
         pltpu.VMEM((micro, 2, rows, 256), F32),
         pltpu.VMEM((4, 8, 64, 256), BF),
@@ -1151,15 +1156,16 @@
         pltpu.VMEM((112, 256), BF),
         pltpu.VMEM((64, VPAD), F32),
         pltpu.VMEM((3, 32, VPAD), F32),
-        pltpu.VMEM((3, 32, VPAD), F32),
+        pltpu.VMEM((2, 32, VPAD), F32),
         pltpu.VMEM((3, 32, VPAD), F32),
         pltpu.VMEM((64, VPAD), F32),
+        pltpu.VMEM((32, VPAD), F32),
         pltpu.VMEM((32, VPAD), F32),
         pltpu.VMEM((32, VPAD), F32),
     ]
     shapes = [
         (3,), (4,), (3, 2), (4, 2), (8, 2), (16, 2), (3,), (4,), (8,), (16,),
-        (steps, 2, 3, 2), (n, 2), (steps, 2), (steps, 2, 3, 2),
+        (steps, 2, 3, 2), (n, 2), (steps, 2),
         (steps, 2, 2, 2), (steps, 2, 2), (3,), (4,), (11,), (10,), (6,), (3,),
     ]
     for shape in shapes:

time: 248 us -> 240 us (0.968)
  Pallas kernels: 243 us -> 237 us
    pallas_call x1, Pallas kernels: 239 us -> 233 us  [fused(): pl.pallas_call(functools.partial(lstm_kernel, steps, rows), out_shape=(ja...]
where the time goes in v2:
time: 240 us
  Pallas kernels  237 us (99%)
  between operations  2.43 us (1%)
    pallas_call x1, Pallas kernels, fused(): pl.pallas_call(functools.partial(lstm_kernel, steps, rows), out_shape=(ja...  233 us

profile of v2, /device:TPU:13, one launch (start us, length us, event | category | flops | bytes accessed | tf_op | source)
XLA Modules:
  0.0 239.5 jit_solution(3326256531639367387)
XLA Ops:
  0.6 233.4 %shard_map.152 = (f32[8,64,256]{2,1,0:T(8,128)}, bf16[3,8,64,256]{3,2,1,0:T(8,128)(2,1)}, f32[104,256]{1,0:T(8,128)}, f32[64,384]{1,0:T(8,128)}, bf16[12,32,2048]{2,1,0:T(8,128)(2,1)}, /*index=5*/f32[128,384]{1,0:T(8,128)}) custom-call(bf16[64,8192]{1,0:T(8,128)(2,1)} %w_rec.1, bf16[100,256]{1,0:T(8,128)(2,1)} %w_in_raw.1, bf16[256]{0:T(256)(128)(2,1)} %b_in_raw.1, ...), custom_call_target="tpu_custom_call" | custom-call | tf_op jit(solution)/shard_map/pallas_call | solution.py:1174
  234.0 3.7 %shard_map.153 = (bf16[12,32,2048]{2,1,0:T(8,128)(2,1)}, f32[275,100]{1,0:T(8,128)}, f32[100,256]{1,0:T(8,128)}, f32[256]{0:T(256)}, f32[64,8192]{1,0:T(8,128)},...) custom-call(f32[8,64,256]{2,1,0:T(8,128)} %get-tuple-element.22.own, ...), custom_call_target="tpu_custom_call" | custom-call | tf_op jit(solution)/shard_map/pallas_call | solution.py:1195

commit v3 on v2

--- a/solution.py
+++ b/solution.py
@@ -30,10 +30,10 @@
 
 def lstm_kernel(
     steps, rows,
-    w_rec, w_in_raw, b_in_raw, w_dec_raw, emb_raw, bias_raw, chars_in, resets_in, targets_in,
+    w_rec, w_in_hbm, b_in_hbm, w_dec_hbm, emb_hbm, bias_hbm, chars_hbm, resets_hbm, targets_hbm,
     out_own, out_recv, out_in, out_dec, out_hid, out_small,
     W, WIN, WDEC, IDS, H, HT, HTS, HSEND, A, C, D, DS, DRAW, DL,
-    ids_in, w_in, emb_t, w_dec, bias_dec, PR, STG, CB, PEND, OWN, DCN, SY, RY, SM, RM, EMBT, LV, BD, GWD, GIS, GY, GM, DWI, SIY, IY, SIM, IM, RS1, RS2, RS3, RS4, RS5, PIECE, PAIR, TOTAL,
+    w_in_raw, b_in_raw, w_dec_raw, emb_raw, bias_raw, chars_in, resets_in, targets_in, load_sem, ids_in, w_in, emb_t, w_dec, bias_dec, PR, STG, CB, PEND, OWN, DCN, SY, RY, SM, RM, EMBT, LV, BD, GWD, GIS, GY, SGM, GM, DWI, SIY, IY, SIM, IM, RS1, RS2, RS3, RS4, RS5, PIECE, PAIR, TOTAL,
     s_ids, r_ids, s_win, r_win, s_wa, r_wa, s_wm, r_wm, s_wy, r_wy, s_ws, r_ws,
     s_da, r_da, s_dm, r_dm, s_dy, r_dy, s_ds, r_ds, s_h, r_h, s_ht, r_ht, s_d, r_d,
     s_ph, r_ph, s_cb, r_cb, s_gd, r_gd, s_gi, r_gi, s_sm, r_sm, s_ry, r_ry, s_rm, r_rm, s_ra, r_ra,
@@ -87,6 +87,30 @@
             src_ref=src, dst_ref=dst, send_sem=ss, recv_sem=rs, device_id=to, device_id_type=MESH
         )
 
+    barrier = pltpu.get_barrier_semaphore()
+
+    def greet(to):
+        pl.semaphore_signal(barrier, inc=1, device_id=to, device_id_type=MESH)
+
+    for k in (1, 2, 3):
+        greet(kdev(k))
+    for to in (mir, ydev, sib):
+        greet(to)
+
+    @pl.when(moved)
+    def _():
+        greet(perm)
+        greet(back)
+
+    pairs = (
+        (w_in_hbm, w_in_raw), (b_in_hbm, b_in_raw), (w_dec_hbm, w_dec_raw), (emb_hbm, emb_raw), (bias_hbm, bias_raw),
+        (chars_hbm, chars_in), (resets_hbm, resets_in), (targets_hbm, targets_in),
+    )
+    loads = [pltpu.make_async_copy(src, dst, load_sem.at[n]) for n, (src, dst) in enumerate(pairs)]
+    for load in loads:
+        load.start()
+    for load in loads:
+        load.wait()
     emb, vocab = emb_raw.shape[1], emb_raw.shape[0]
     w_in[...] = jnp.zeros_like(w_in)
     w_in[0:emb, :] = w_in_raw[...]
@@ -102,21 +126,6 @@
         ).astype(F32)
         wide_stack = jnp.concatenate([stack, jnp.zeros((24, 96), F32)], axis=1)
         ids_in[s] = wide_stack.T[:32, :].astype(jnp.int32)
-    barrier = pltpu.get_barrier_semaphore()
-
-    def greet(to):
-        pl.semaphore_signal(barrier, inc=1, device_id=to, device_id_type=MESH)
-
-    for k in (1, 2, 3):
-        greet(kdev(k))
-    for to in (mir, ydev, sib):
-        greet(to)
-
-    @pl.when(moved)
-    def _():
-        greet(perm)
-        greet(back)
-
     pl.semaphore_wait(barrier, 6 + 2 * moved.astype(jnp.int32))
 
 
@@ -622,7 +631,7 @@
         return rc(GWD.at[:, 1 - y, c], GY, s_gd.at[1], r_gd.at[1], ydev)
 
     def gd_m():
-        return rc(GWD.at[1 - zh, y, c], GM, s_gd.at[2], r_gd.at[2], mir)
+        return rc(SGM, GM, s_gd.at[2], r_gd.at[2], mir)
 
     turn()
 
@@ -645,13 +654,12 @@
         def _():
             add_owed(t + 1 - s, 1 - s)
 
+        @pl.when(i >= 2)
+        def _():
+            pr_left(t + 1, s)
+
+        product_back(t, s)
         d_copy(t, s).start()
-
-        @pl.when(i >= 2)
-        def _():
-            pr_left(t + 1, s)
-
-        product_back(t, s)
 
         @pl.when(i < 2 * (steps - 1) - 1)
         def _():
@@ -684,12 +692,13 @@
         def _():
             gd_y().wait_recv()
             GWD[:, y, c] += GY[...]
+            SGM[...] = GWD[1 - zh, y, c].astype(BF)
             gd_m().start()
 
         @pl.when(i == 9)
         def _():
             gd_m().wait_recv()
-            out_dec[...] = GWD[zh, y, c] + GM[...]
+            out_dec[...] = GWD[zh, y, c] + GM[...].astype(F32)
 
     @pl.loop(0, 2 * (steps - 1))
     def _(i):
@@ -708,37 +717,37 @@
     def ry_copy(p, q):
         return rc(SY.at[p % 4], RY.at[q], s_ry.at[p], r_ry.at[q], ydev)
 
-    def rm_copy(k):
-        return rc(SM.at[k], RM.at[k], s_rm.at[k], r_rm.at[k], mir)
-
-    def half(h):
-        return pl.ds(4 * h, 4)
-
-    def ry_half(h):
-        return rc(SY.at[0, half(h)], RY.at[3, half(h)], s_ry.at[8 + h], r_ry.at[8 + h], ydev)
-
-    def rm_half(h):
-        return rc(SM.at[3, half(h)], RM.at[3, half(h)], s_rm.at[4 + h], r_rm.at[4 + h], mir)
+    def pieces(k):
+        return (1, 2, 1, 4)[k]
+
+    def piece(k, n):
+        size = 8 // pieces(k)
+        return slice(size * n, size * (n + 1))
+
+    def rm_copy(k, n):
+        at = (0, 2, 1, 4)[k] + n
+        return rc(SM.at[k, piece(k, n)], RM.at[k, piece(k, n)], s_rm.at[at], r_rm.at[at], mir)
+
+    def ry_first(n):
+        return rc(SY.at[0, piece(3, n)], RY.at[3, piece(3, n)], s_ry.at[8 + n], r_ry.at[8 + n], ydev)
 
     def ry_sent(p):
         @pl.when(p == 0)
         def _():
-            ry_half(0).wait_send()
-            ry_half(1).wait_send()
+            for n in range(4):
+                ry_first(n).wait_send()
 
         @pl.when(p > 0)
         def _():
             ry_copy(p, order(p)).wait_send()
 
-    def rm_sent(k):
-        if k == 3:
-            rm_half(0).wait_send()
-            rm_half(1).wait_send()
-        else:
-            rm_copy(k).wait_send()
-
-    def ra_copy(k):
-        return rc(SM.at[k], out_recv.at[k - 1], s_ra.at[k - 1], r_ra.at[k - 1], kdev(k))
+    def ra_copy(k, n):
+        at = (0, 0, 2, 3)[k] + n
+        rows_of_q = piece(k, n) if k == 1 else slice(0, 8)
+        return rc(SM.at[k, rows_of_q], out_recv.at[k - 1, rows_of_q], s_ra.at[at], r_ra.at[at], kdev(k))
+
+    def ra_pieces(k):
+        return 2 if k == 1 else 1
 
     def order(p):
         return 3 - p + 8 * (p // 4)
@@ -757,10 +766,10 @@
             grad = mm(left, D[n].reshape(depth, 256), NN) + mm(right, DS[n].reshape(depth, 256), NN)
             hold[n] = grad[:64]
             SY[p % 4, n] = grad[64:].astype(BF)
-            if n % 4 == 3:
+            if n % 2 == 1:
                 @pl.when(p == 0)
                 def _(n=n):
-                    ry_half(n // 4).start()
+                    ry_first(n // 2).start()
 
         @pl.when(p > 0)
         def _():
@@ -771,29 +780,39 @@
         hold = kept(q)
         hold[...] = hold[...] + RY[q].astype(F32)
 
+    def pass_first(n):
+        ry_first(n).wait_recv()
+        SM[3, piece(3, n)] = (kept(3)[piece(3, n)] + RY[3, piece(3, n)].astype(F32)).astype(BF)
+        rm_copy(3, n).start()
+
     def pass_on(k):
         if k == 3:
-            for h in (0, 1):
-                pass_half(h)
+            for n in range(4):
+                pass_first(n)
             return
         add_y(k)
-        SM[k] = kept(k)[...].astype(BF)
-        rm_copy(k).start()
+        for n in range(pieces(k)):
+            SM[k, piece(k, n)] = kept(k)[piece(k, n)].astype(BF)
+            rm_copy(k, n).start()
 
     def finish(k):
         add_y(4 + k)
-        if k == 3:
-            rm_half(0).wait_recv()
-            rm_half(1).wait_recv()
-        else:
-            rm_copy(k).wait_recv()
-        total = kept(4 + k)[...] + RM[k].astype(F32)
+        if k != 1:
+            for n in range(pieces(k)):
+                rm_copy(k, n).wait_recv()
         if k == 0:
-            out_own[...] = total
-        else:
-            rm_sent(k)
-            SM[k] = total.astype(BF)
-            ra_copy(k).start()
+            out_own[...] = kept(4)[...] + RM[0].astype(F32)
+            return
+        for n in range(ra_pieces(k)):
+            part = piece(1, n) if k == 1 else slice(0, 8)
+            if k == 1:
+                rm_copy(k, n).wait_recv()
+                rm_copy(k, n).wait_send()
+            else:
+                for m in range(pieces(k)):
+                    rm_copy(k, m).wait_send()
+            SM[k, part] = (kept(4 + k)[part] + RM[k, part].astype(F32)).astype(BF)
+            ra_copy(k, n).start()
 
     def settle(p):
         q = order(p)
@@ -895,11 +914,6 @@
 
     def gi_p():
         return rc(DWI.at[y, zh, c, live], out_in, s_gi.at[3], r_gi.at[3], back)
-
-    def pass_half(h):
-        ry_half(h).wait_recv()
-        SM[3, half(h)] = (kept(3)[half(h)] + RY[3, half(h)].astype(F32)).astype(BF)
-        rm_half(h).start()
 
     def first_position():
         @pl.loop(0, 2)
@@ -910,7 +924,7 @@
 
             @pl.when(jnp.logical_and(inner, s == 0))
             def _():
-                pass_half(0)
+                pass_first(2)
 
         leader = jnp.logical_and(x == 0, a == 0)
         high_row = lax.broadcasted_iota(jnp.int32, (8, VPAD), 0)
@@ -932,12 +946,21 @@
 
         @pl.when(p == 1)
         def _():
+            @pl.when(inner)
+            def _():
+                pass_first(0)
+
             input_side(1, 1)
+
+            @pl.when(inner)
+            def _():
+                pass_first(1)
+
             first_position()
             sm_step1()
             @pl.when(inner)
             def _():
-                pass_half(1)
+                pass_first(3)
                 settle(1)
 
             gi_s().wait_recv()
@@ -997,8 +1020,9 @@
             wa(k, j).wait_send()
         ids_copy(k, member(0)).wait_send()
         da(k).wait_send()
-        ra_copy(k).wait()
-    rm_copy(0).wait_send()
+        for n in range(ra_pieces(k)):
+            ra_copy(k, n).wait()
+    rm_copy(0, 0).wait_send()
 
     @pl.when(moved)
     def _():
@@ -1127,6 +1151,15 @@
         pltpu.VMEM((8, n, micro, rows, 256), BF),
         pltpu.VMEM((8, rows, 256), BF),
         pltpu.VMEM((steps, micro, rows, VPAD), BF),
+        pltpu.VMEM(w_in.shape, BF),
+        pltpu.VMEM(bias_in.shape, BF),
+        pltpu.VMEM(w_dec.shape, BF),
+        pltpu.VMEM(embed.shape, BF),
+        pltpu.VMEM(bias_dec.shape, BF),
+        pltpu.VMEM((steps, micro, count), jnp.int32),
+        pltpu.VMEM((steps, micro, count), jnp.int32),
+        pltpu.VMEM((steps, micro, count), jnp.int32),
+        dma((8,)),
         pltpu.VMEM((micro, count, 24), jnp.int32),
         pltpu.VMEM((EPAD, 256), BF),
         pltpu.VMEM((EPAD, VPAD), BF),
@@ -1148,7 +1181,8 @@
         pltpu.VMEM((2, 2, 2, 64, VPAD), F32),
         pltpu.VMEM((2, 2, 104, VPAD), F32),
         pltpu.VMEM((2, 64, VPAD), F32),
-        pltpu.VMEM((64, VPAD), F32),
+        pltpu.VMEM((64, VPAD), BF),
+        pltpu.VMEM((64, VPAD), BF),
         pltpu.VMEM((2, 2, 2, EPAD, 256), F32),
         pltpu.VMEM((2, 112, 256), BF),
         pltpu.VMEM((2, 112, 256), BF),
@@ -1166,7 +1200,7 @@
     shapes = [
         (3,), (4,), (3, 2), (4, 2), (8, 2), (16, 2), (3,), (4,), (8,), (16,),
         (steps, 2, 3, 2), (n, 2), (steps, 2),
-        (steps, 2, 2, 2), (steps, 2, 2), (3,), (4,), (11,), (10,), (6,), (3,),
+        (steps, 2, 2, 2), (steps, 2, 2), (3,), (4,), (11,), (12,), (8,), (4,),
     ]
     for shape in shapes:
         scratch += [dma(shape), dma(shape)]
@@ -1181,7 +1215,7 @@
             jax.ShapeDtypeStruct((micro * steps, count, width), BF),
             jax.ShapeDtypeStruct((EPAD, VPAD), F32),
         ),
-        in_specs=[hbm] + [vm] * 8,
+        in_specs=[hbm] * 9,
         out_specs=(vm, hbm, vm, vm, hbm, vm),
         scratch_shapes=scratch,
         compiler_params=pltpu.CompilerParams(

time: 240 us -> 235 us (0.979)
  Pallas kernels: 237 us -> 233 us
    pallas_call x1, Pallas kernels: 233 us -> 229 us  [fused(): pl.pallas_call(functools.partial(lstm_kernel, steps, rows), out_shape=(ja...]
where the time goes in v3:
time: 235 us
  Pallas kernels  233 us (99%)
  between operations  2.43 us (1%)
    pallas_call x1, Pallas kernels, fused(): pl.pallas_call(functools.partial(lstm_kernel, steps, rows), out_shape=(ja...  229 us

profile of v3, /device:TPU:13, one launch (start us, length us, event | category | flops | bytes accessed | tf_op | source)
XLA Modules:
  0.0 234.9 jit_solution(16872298353587446994)
XLA Ops:
  0.6 228.8 %shard_map.152 = (f32[8,64,256]{2,1,0:T(8,128)}, bf16[3,8,64,256]{3,2,1,0:T(8,128)(2,1)}, f32[104,256]{1,0:T(8,128)}, f32[64,384]{1,0:T(8,128)}, bf16[12,32,2048]{2,1,0:T(8,128)(2,1)}, /*index=5*/f32[128,384]{1,0:T(8,128)}) custom-call(bf16[64,8192]{1,0:T(8,128)(2,1)} %w_rec.1, bf16[100,256]{1,0:T(8,128)(2,1)} %w_in_hbm.1, bf16[256]{0:T(256)(128)(2,1)} %b_in_hbm.1, ...), custom_call_target="tpu_custom_call" | custom-call | tf_op jit(solution)/shard_map/pallas_call | solution.py:1208
  229.5 3.7 %shard_map.153 = (bf16[12,32,2048]{2,1,0:T(8,128)(2,1)}, f32[275,100]{1,0:T(8,128)}, f32[100,256]{1,0:T(8,128)}, f32[256]{0:T(256)}, f32[64,8192]{1,0:T(8,128)},...) custom-call(f32[8,64,256]{2,1,0:T(8,128)} %get-tuple-element.22.own, ...), custom_call_target="tpu_custom_call" | custom-call | tf_op jit(solution)/shard_map/pallas_call | solution.py:1229

commit v4 on v3

--- a/solution.py
+++ b/solution.py
@@ -718,26 +718,34 @@
         return rc(SY.at[p % 4], RY.at[q], s_ry.at[p], r_ry.at[q], ydev)
 
     def pieces(k):
-        return (1, 2, 1, 4)[k]
+        return (1, 2, 2, 4)[k]
 
     def piece(k, n):
         size = 8 // pieces(k)
         return slice(size * n, size * (n + 1))
 
     def rm_copy(k, n):
-        at = (0, 2, 1, 4)[k] + n
+        at = (0, 1, 3, 5)[k] + n
         return rc(SM.at[k, piece(k, n)], RM.at[k, piece(k, n)], s_rm.at[at], r_rm.at[at], mir)
 
     def ry_first(n):
         return rc(SY.at[0, piece(3, n)], RY.at[3, piece(3, n)], s_ry.at[8 + n], r_ry.at[8 + n], ydev)
 
+    def ry_second(n):
+        return rc(SY.at[1, piece(2, n)], RY.at[2, piece(2, n)], s_ry.at[12 + n], r_ry.at[12 + n], ydev)
+
     def ry_sent(p):
         @pl.when(p == 0)
         def _():
             for n in range(4):
                 ry_first(n).wait_send()
 
-        @pl.when(p > 0)
+        @pl.when(p == 1)
+        def _():
+            for n in range(2):
+                ry_second(n).wait_send()
+
+        @pl.when(p > 1)
         def _():
             ry_copy(p, order(p)).wait_send()
 
@@ -771,7 +779,12 @@
                 def _(n=n):
                     ry_first(n // 2).start()
 
-        @pl.when(p > 0)
+            if n % 4 == 3:
+                @pl.when(p == 1)
+                def _(n=n):
+                    ry_second(n // 4).start()
+
+        @pl.when(p > 1)
         def _():
             ry_copy(p, q).start()
 
@@ -789,6 +802,12 @@
         if k == 3:
             for n in range(4):
                 pass_first(n)
+            return
+        if k == 2:
+            for n in range(2):
+                ry_second(n).wait_recv()
+                SM[2, piece(2, n)] = (kept(2)[piece(2, n)] + RY[2, piece(2, n)].astype(F32)).astype(BF)
+                rm_copy(2, n).start()
             return
         add_y(k)
         for n in range(pieces(k)):
@@ -1200,7 +1219,7 @@
     shapes = [
         (3,), (4,), (3, 2), (4, 2), (8, 2), (16, 2), (3,), (4,), (8,), (16,),
         (steps, 2, 3, 2), (n, 2), (steps, 2),
-        (steps, 2, 2, 2), (steps, 2, 2), (3,), (4,), (11,), (12,), (8,), (4,),
+        (steps, 2, 2, 2), (steps, 2, 2), (3,), (4,), (11,), (14,), (9,), (4,),
     ]
     for shape in shapes:
         scratch += [dma(shape), dma(shape)]

time: 235 us -> 234 us (level)
  no operation moved by 1% of the time
where the time goes in v4:
time: 234 us
  Pallas kernels  231 us (99%)
  between operations  2.43 us (1%)
    pallas_call x1, Pallas kernels, fused(): pl.pallas_call(functools.partial(lstm_kernel, steps, rows), out_shape=(ja...  227 us

profile of v4, /device:TPU:13, one launch (start us, length us, event | category | flops | bytes accessed | tf_op | source)
XLA Modules:
  0.0 233.6 jit_solution(3131749975152404043)
XLA Ops:
  0.6 227.5 %shard_map.152 = (f32[8,64,256]{2,1,0:T(8,128)}, bf16[3,8,64,256]{3,2,1,0:T(8,128)(2,1)}, f32[104,256]{1,0:T(8,128)}, f32[64,384]{1,0:T(8,128)}, bf16[12,32,2048]{2,1,0:T(8,128)(2,1)}, /*index=5*/f32[128,384]{1,0:T(8,128)}) custom-call(bf16[64,8192]{1,0:T(8,128)(2,1)} %w_rec.1, bf16[100,256]{1,0:T(8,128)(2,1)} %w_in_hbm.1, bf16[256]{0:T(256)(128)(2,1)} %b_in_hbm.1, ...), custom_call_target="tpu_custom_call" | custom-call | tf_op jit(solution)/shard_map/pallas_call | solution.py:1227
  228.1 3.7 %shard_map.153 = (bf16[12,32,2048]{2,1,0:T(8,128)(2,1)}, f32[275,100]{1,0:T(8,128)}, f32[100,256]{1,0:T(8,128)}, f32[256]{0:T(256)}, f32[64,8192]{1,0:T(8,128)},...) custom-call(f32[8,64,256]{2,1,0:T(8,128)} %get-tuple-element.22.own, ...), custom_call_target="tpu_custom_call" | custom-call | tf_op jit(solution)/shard_map/pallas_call | solution.py:1248

commit v5 on v4

--- a/solution.py
+++ b/solution.py
@@ -1090,7 +1090,7 @@
 
 
 def output_kernel(
-    own, recv, g_in, g_dec, hid_in, small, hid, table, o_in, o_bias, o_rec, o_dec, o_bias_dec, loss,
+    characters, own, recv, g_in, g_dec, hid_in, small, hid, table, o_in, o_bias, o_rec, o_dec, o_bias_dec, loss,
     h_buf, own_buf, recv_buf, rec_buf, in_buf, dec_buf, small_buf, t_buf, i_buf, b_buf, d_buf, bd_buf, l_buf, in_sem, out_sem,
 ):
     dp = lax.axis_index("dp")
@@ -1136,7 +1136,7 @@
     b_buf[...] = in_buf[emb, :]
     d_buf[...] = dec_buf[:, :vocab]
     bd_buf[...] = small_buf[SMALL - 8, :vocab]
-    l_buf[...] = small_buf[SMALL - 7 : SMALL - 6, 0:1]
+    l_buf[...] = small_buf[SMALL - 7 : SMALL - 6, 0:1] / characters
     pairs = ((t_buf, table), (i_buf, o_in), (b_buf, o_bias), (d_buf, o_dec), (bd_buf, o_bias_dec), (l_buf, loss))
     for n, (src, dst) in enumerate(pairs):
         stores.append(store(2 + n, src, dst))
@@ -1246,7 +1246,7 @@
     )
     everyone = lax.axis_size(("dp", "fsdp"))
     hid, table, g_in, g_bias, g_rec, g_dec, g_bias_dec, loss = pl.pallas_call(
-        output_kernel,
+        functools.partial(output_kernel, float(micro * count * steps * everyone)),
         out_shape=(
             jax.ShapeDtypeStruct((micro * steps, count, width), BF),
             jax.ShapeDtypeStruct((vocab, emb), F32),
@@ -1278,7 +1278,7 @@
         ],
     )(out_own, out_recv, out_in, out_dec, out_hid, out_small)
     return (
-        loss[0, 0] / (micro * count * steps * everyone),
+        loss.reshape(()),
         hid.reshape(micro, steps, count, width).transpose(0, 2, 1, 3),
         table,
         g_in,

time: 234 us -> 232 us (level)
  no operation moved by 1% of the time
where the time goes in v5:
time: 232 us
  Pallas kernels  231 us (100%)
    pallas_call x1, Pallas kernels, fused(): pl.pallas_call(functools.partial(lstm_kernel, steps, rows), out_shape=(ja...  227 us

profile of v5, /device:TPU:13, one launch (start us, length us, event | category | flops | bytes accessed | tf_op | source)
XLA Modules:
  0.0 232.0 jit_solution(1723035877810215846)
XLA Ops:
  0.6 227.5 %shard_map.152 = (f32[8,64,256]{2,1,0:T(8,128)}, bf16[3,8,64,256]{3,2,1,0:T(8,128)(2,1)}, f32[104,256]{1,0:T(8,128)}, f32[64,384]{1,0:T(8,128)}, bf16[12,32,2048]{2,1,0:T(8,128)(2,1)}, /*index=5*/f32[128,384]{1,0:T(8,128)}) custom-call(bf16[64,8192]{1,0:T(8,128)(2,1)} %w_rec.1, bf16[100,256]{1,0:T(8,128)(2,1)} %w_in_hbm.1, bf16[256]{0:T(256)(128)(2,1)} %b_in_hbm.1, ...), custom_call_target="tpu_custom_call" | custom-call | tf_op jit(solution)/shard_map/pallas_call | solution.py:1227
  228.1 3.7 %shard_map.153 = (bf16[12,32,2048]{2,1,0:T(8,128)(2,1)}, f32[275,100]{1,0:T(8,128)}, f32[100,256]{1,0:T(8,128)}, f32[256]{0:T(256)}, f32[64,8192]{1,0:T(8,128)},...) custom-call(f32[8,64,256]{2,1,0:T(8,128)} %get-tuple-element.22.own, ...), custom_call_target="tpu_custom_call" | custom-call | tf_op jit(solution)/shard_map/pallas_call | solution.py:1248

commit v6 on v5

--- a/solution.py
+++ b/solution.py
@@ -389,12 +389,10 @@
         return rc(d_slot(b), d_slot(b), s_ds.at[i], r_ds.at[i], sib)
 
     own_dec.wait()
-    dec_mir(0, 0).start()
     dec_y(0, y).start()
     dec_s(0, c).start()
     for k in (1, 2, 3):
         da(k).wait_recv()
-        dec_mir(k, 0).start()
         dec_y(k, y).start()
         dec_s(k, c).start()
 
@@ -508,7 +506,13 @@
         t, s = i // 2, i % 2
         forward(t, s)
 
-        @pl.when(i == 3)
+        @pl.when(i == 2)
+        def _():
+            @pl.loop(0, 4)
+            def _(k):
+                dec_mir(k, 0).start()
+
+        @pl.when(i == 4)
         def _():
             decoder_mirror()
 

time: 232 us -> 236 us (1.017)
  Pallas kernels: 231 us -> 235 us
    pallas_call x1, Pallas kernels: 227 us -> 231 us  [fused(): pl.pallas_call(functools.partial(lstm_kernel, steps, rows), out_shape=(ja...]
where the time goes in v6:
time: 236 us; the launch traced here: 235 us
  Pallas kernels  235 us (100%)
    pallas_call x1, Pallas kernels, fused(): pl.pallas_call(functools.partial(lstm_kernel, steps, rows), out_shape=(ja...  231 us

profile of v6, /device:TPU:13, one launch (start us, length us, event | category | flops | bytes accessed | tf_op | source)
XLA Modules:
  0.0 235.5 jit_solution(13590422033701928362)
XLA Ops:
  0.6 231.0 %shard_map.152 = (f32[8,64,256]{2,1,0:T(8,128)}, bf16[3,8,64,256]{3,2,1,0:T(8,128)(2,1)}, f32[104,256]{1,0:T(8,128)}, f32[64,384]{1,0:T(8,128)}, bf16[12,32,2048]{2,1,0:T(8,128)(2,1)}, /*index=5*/f32[128,384]{1,0:T(8,128)}) custom-call(bf16[64,8192]{1,0:T(8,128)(2,1)} %w_rec.1, bf16[100,256]{1,0:T(8,128)(2,1)} %w_in_hbm.1, bf16[256]{0:T(256)(128)(2,1)} %b_in_hbm.1, ...), custom_call_target="tpu_custom_call" | custom-call | tf_op jit(solution)/shard_map/pallas_call | solution.py:1231
  231.6 3.7 %shard_map.153 = (bf16[12,32,2048]{2,1,0:T(8,128)(2,1)}, f32[275,100]{1,0:T(8,128)}, f32[100,256]{1,0:T(8,128)}, f32[256]{0:T(256)}, f32[64,8192]{1,0:T(8,128)},...) custom-call(f32[8,64,256]{2,1,0:T(8,128)} %get-tuple-element.22.own, ...), custom_call_target="tpu_custom_call" | custom-call | tf_op jit(solution)/shard_map/pallas_call | solution.py:1252
